TPU v7x, 128 devices: a whole 4x4x4 slice. The times are simulated.
128 devices in a mesh: row: 8 (over z, core), col: 16 (over y, x).
Axes of the slice: x: 4, y: 4, z: 4, core: 2. Of those that a mesh axis runs over, the one named last changes fastest.
Arguments:
- stiffness_blocks: float32 [1024, 20, 4096], P(('row', 'col')), as said below
- block_columns: int32 [1024, 20], P(('row', 'col')), may hold values from 0 to 7, as said below
- block_counts: int32 [1024, 5], P(('row', 'col')), may hold values from 0 to 4, as said below
- tentative_tiles: float32 [1024, 4096], P(('row', 'col')), may hold values from -1.5 to 1.5
- aggregate_of: int32 [1024], replicated, may hold values from 0 to 255, as said below
Outputs:
- coarse_operator: float32 [256, 64, 1664], P(('row', 'col'))
Inputs may be any that keep to these rules, and one draw needn't show every extreme that they name: `block_columns`: the slots of one row in one class name different blocks; slot 0 names the row's own block, I % 8. `block_counts`: class 0 has 1 or more live slots; a class whose step leaves the grid has none; every device holds a row with 4 live slots in each class whose step stays in the grid. `aggregate_of`: the fine blocks of device d go to aggregates d * 2 to (d + 1) * 2 - 1, exactly 4 to each. `stiffness_blocks`: the diagonal entries of every row's slot 0 block lie between 2 and 10.
All inputs are finite; a program needn't handle non-finite values.
Results may differ from a plain program's by a relative error of at most 0.0003.
Values sent between devices are 32-bit elements; how exact they have to be, the bound alone decides.
A program may use at most 128 MiB of HBM per device.

v0:
```python
import jax
import jax.numpy as jnp
from jax import lax
from jax.sharding import PartitionSpec as P

FINE_DOF = 64
COARSE_DOF = 64
ROW_SLOTS = 4
NEIGHBORS = 5
OFFSETS = 13
AGG_DEV = 2
AGGS_NEAR = 10


OMEGA = 2.0 / 3.0
HIGHEST = lax.Precision.HIGHEST
CLASS_STEPS = ((0, 0), (0, -1), (0, 1), (-1, 0), (1, 0))
BAND_STEPS = (
    (-2, 0),
    (-1, -1),
    (-1, 0),
    (-1, 1),
    (0, -2),
    (0, -1),
    (0, 0),
    (0, 1),
    (0, 2),
    (1, -1),
    (1, 0),
    (1, 1),
    (2, 0),
)
HALO_PLACES = (4, 3, 5, 1, 7)


def padded(x, sides, width):
    for axis, dim in sides:
        devices, length = (lax.axis_size(axis), x.shape[dim])
        up = [(i, (i + 1) % devices) for i in range(devices - 1)]
        down = [(j, i) for i, j in up]
        last = lax.slice_in_dim(x, length - width, length, axis=dim)
        leading = lax.slice_in_dim(x, 0, width, axis=dim)
        before = lax.ppermute(last, axis, up)
        after = lax.ppermute(leading, axis, down)
        x = jnp.concatenate([before, x, after], axis=dim)
    return x


def from_behind(x, axis, by):
    devices = lax.axis_size(axis)
    pairs = [(i, i + by) for i in range(devices) if 0 <= i + by < devices]
    return lax.ppermute(x, axis, pairs)


def coarse_rows(left_side, right_side):
    return lax.dot_general(left_side, right_side, (((0,), (0,)), ((), ())), precision=HIGHEST)


def body(stiffness_blocks, block_columns, block_counts, tentative_tiles, aggregate_of):
    rows_here = stiffness_blocks.shape[0]
    slot_count = stiffness_blocks.shape[1]
    row_count = lax.axis_size("row")
    col_count = lax.axis_size("col")
    grid_row = lax.axis_index("row")
    grid_col = lax.axis_index("col")
    row_steps = jnp.array([class_step[0] for class_step in CLASS_STEPS], dtype=jnp.int32)
    col_steps = jnp.array([class_step[1] for class_step in CLASS_STEPS], dtype=jnp.int32)
    halo_places = jnp.array(HALO_PLACES, dtype=jnp.int32)
    near_device = jnp.clip(grid_row + row_steps, 0, row_count - 1) * col_count + jnp.clip(
        grid_col + col_steps, 0, col_count - 1
    )
    class_of = jnp.arange(slot_count, dtype=jnp.int32) // ROW_SLOTS
    within = jnp.arange(slot_count, dtype=jnp.int32) % ROW_SLOTS
    spread = padded(
        tentative_tiles.reshape(1, 1, rows_here, FINE_DOF * COARSE_DOF), (("row", 0), ("col", 1)), 1
    )
    near_tiles = spread.reshape(9 * rows_here, FINE_DOF, COARSE_DOF)
    live_mask = within[None, :] < jnp.take(block_counts, class_of, axis=1)
    blocks = jnp.where(live_mask[:, :, None], stiffness_blocks, 0.0).reshape(
        rows_here, slot_count, FINE_DOF, FINE_DOF
    )
    picked = jnp.take(
        near_tiles, halo_places[class_of][None, :] * rows_here + block_columns, axis=0
    )
    stiff_tent = jnp.einsum("ksab,ksbc->ksac", blocks, picked, precision=HIGHEST)
    damping = OMEGA / jnp.diagonal(blocks[:, 0], axis1=1, axis2=2)
    own_tiles = tentative_tiles.reshape(rows_here, FINE_DOF, COARSE_DOF)
    diagonal_slot = jnp.arange(slot_count, dtype=jnp.int32) == 0
    smoothed = (
        jnp.where(diagonal_slot[None, :, None, None], own_tiles[:, None], 0.0)
        - damping[:, None, :, None] * stiff_tent
    )
    fine_index = near_device[class_of][None, :] * rows_here + block_columns
    coarse_ids = jnp.take(aggregate_of, fine_index, axis=0)
    local_ids = class_of[None, :] * AGG_DEV + coarse_ids % AGG_DEV
    member = (
        local_ids[:, :, None] == jnp.arange(AGGS_NEAR, dtype=jnp.int32)[None, None, :]
    ).astype(jnp.float32)
    tile_width = AGG_DEV * COARSE_DOF
    flat_width = FINE_DOF * COARSE_DOF
    left_grouped = jnp.einsum(
        "ksg,ksm->kgm",
        member,
        smoothed.reshape(rows_here, slot_count, flat_width),
        precision=HIGHEST,
    )
    right_grouped = jnp.einsum(
        "ksg,ksm->kgm",
        member,
        stiff_tent.reshape(rows_here, slot_count, flat_width),
        precision=HIGHEST,
    )
    left_side = jnp.transpose(
        left_grouped.reshape(rows_here, NEIGHBORS, AGG_DEV, FINE_DOF, COARSE_DOF), (1, 0, 3, 2, 4)
    ).reshape(NEIGHBORS, rows_here * FINE_DOF, tile_width)
    right_side = jnp.transpose(
        right_grouped.reshape(rows_here, AGGS_NEAR, FINE_DOF, COARSE_DOF), (0, 2, 1, 3)
    ).reshape(rows_here * FINE_DOF, NEIGHBORS * tile_width)
    pieces = [coarse_rows(left_side[0], right_side)]
    for source, shift_by in ((1, -1), (2, 1)):
        left_arrived, right_arrived = from_behind((left_side[source], right_side), "col", shift_by)
        pieces.append(coarse_rows(left_arrived, right_arrived))
    for source, shift_by in ((3, -1), (4, 1)):
        left_arrived, right_arrived = from_behind((left_side[source], right_side), "row", shift_by)
        pieces.append(coarse_rows(left_arrived, right_arrived))
    band_slots = [None] * len(BAND_STEPS)
    for source in range(NEIGHBORS):
        piece = pieces[source].reshape(tile_width, NEIGHBORS, tile_width)
        for target in range(NEIGHBORS):
            offset = (
                CLASS_STEPS[target][0] - CLASS_STEPS[source][0],
                CLASS_STEPS[target][1] - CLASS_STEPS[source][1],
            )
            where_to = BAND_STEPS.index(offset)
            if band_slots[where_to] is None:
                band_slots[where_to] = piece[:, target]
            else:
                band_slots[where_to] = band_slots[where_to] + piece[:, target]
    banded = jnp.stack(band_slots, axis=1)
    return banded.reshape(AGG_DEV, COARSE_DOF, OFFSETS * tile_width)


def solution(mesh):
    placed = (
        P(("row", "col"), None, None),
        P(("row", "col"), None),
        P(("row", "col"), None),
        P(("row", "col"), None),
        P(),
    )
    return jax.shard_map(
        body, mesh=mesh, in_specs=placed, out_specs=P(("row", "col"), None, None), check_vma=False
    )
```

profile of v0, /device:TPU:25, one launch (start us, length us, event | category | flops | bytes accessed | tf_op | source)
XLA Modules:
  0.0 169.9 jit_solution(4281155606372770253)
XLA Ops:
  0.0 2.7 %collective-permute-start.1 = (f32[1,1,8,4096]{3,2,1,0:T(8,128)}, f32[1,1,8,4096]{3,2,1,0:T(8,128)S(1)}, u32[]{:S(2)}, u32[]{:S(2)}) collective-permute-start(f32[1,1,8,4096]{3,2,1,0:T(8,128)} %bitcast.78), channel_id=1, source_target_pairs={{16,0},{32,16},{48,32},{64,48},{80,64},{96,80},{112,96},{17,1},{33... | collective-permute-start | bytes 393224 | tf_op jit(solution)/shard_map/ppermute | solution.py:44
  2.7 3.4 %collective-permute-start = (f32[1,1,8,4096]{3,2,1,0:T(8,128)}, f32[1,1,8,4096]{3,2,1,0:T(8,128)S(1)}, u32[]{:S(2)}, u32[]{:S(2)}) collective-permute-start(f32[1,1,8,4096]{3,2,1,0:T(8,128)} %bitcast.79), channel_id=1, source_target_pairs={{0,16},{16,32},{32,48},{48,64},{64,80},{80,96},{96,112},{1,17},{17... | collective-permute-start | bytes 393224 | tf_op jit(solution)/shard_map/ppermute | solution.py:43
  6.2 0.8 copy.24
  7.6 2.1 %broadcast_select_fusion = f32[8,20,4096]{2,0,1:T(8,128)S(1)} fusion(f32[8,20,4096]{2,0,1:T(8,128)} %param.8, pred[8,20]{0,1:T(8,128)(4,1)S(1)} %fusion.16), kind=kLoop, calls=%fused_computation.12 | loop fusion | flops 655360 | bytes 5243040 | tf_op jit(solution)/shard_map/jit(_where)/select_n | solution.py:79
  9.7 19.5 %copy.25 = f32[8,20,4096]{0,2,1:T(8,128)} copy(f32[8,20,4096]{2,0,1:T(8,128)S(1)} %broadcast_select_fusion) | data formatting | bytes 5242880 | tf_op jit(solution)/shard_map/jit(_where)/select_n | solution.py:79
  29.2 1.8 %slice_bitcast_fusion = f32[8,64,64]{0,2,1:T(8,128)S(1)} fusion(f32[8,20,64,64]{0,3,2,1:T(8,128)} %bitcast.69), kind=kLoop, calls=%fused_computation.11 | loop fusion | bytes 262144 | tf_op jit(solution)/shard_map/squeeze | solution.py:86
  31.0 0.9 gather_fusion.3
  31.9 0.7 gather_fusion.4
  32.7 0.7 gather_fusion
  33.5 0.8 broadcast_in_dim.80
  34.3 23.5 %copy.27 = f32[8,20,64,64]{3,2,1,0:T(8,128)} copy(f32[8,20,64,64]{0,3,2,1:T(8,128)} %bitcast.70) | data formatting | bytes 5242880 | tf_op jit(solution)/shard_map/reshape | solution.py:79
  57.9 1.2 gather_fusion.1
  59.8 4.6 %collective-permute-start.3 = (f32[3,1,8,4096]{3,2,1,0:T(8,128)S(1)}, f32[3,1,8,4096]{3,2,1,0:T(8,128)S(1)}, u32[]{:S(2)}, u32[]{:S(2)}) collective-permute-start(f32[3,1,8,4096]{3,2,1,0:T(8,128)S(1)} %pad_maximum_fusion.1), channel_id=1, source_target_pairs={{1,0},{2,1},{3,2},{4,3},{5,4},{6,5},{7,6},{8,7},{9,8},{10,9},{11,1... | collective-permute-start | bytes 1179656 | tf_op jit(solution)/shard_map/ppermute | solution.py:44
  64.4 2.1 %collective-permute-start.2 = (f32[3,1,8,4096]{3,2,1,0:T(8,128)S(1)}, f32[3,1,8,4096]{3,2,1,0:T(8,128)S(1)}, u32[]{:S(2)}, u32[]{:S(2)}) collective-permute-start(f32[3,1,8,4096]{3,2,1,0:T(8,128)S(1)} %pad_maximum_fusion.1), channel_id=1, source_target_pairs={{0,1},{1,2},{2,3},{3,4},{4,5},{5,6},{6,7},{7,8},{8,9},{9,10},{10,1... | collective-permute-start | bytes 1179656 | tf_op jit(solution)/shard_map/ppermute | solution.py:43
  66.5 6.2 %collective-permute-done.3 = f32[3,1,8,4096]{3,2,1,0:T(8,128)S(1)} collective-permute-done((f32[3,1,8,4096]{3,2,1,0:T(8,128)S(1)}, f32[3,1,8,4096]{3,2,1,0:T(8,128)S(1)}, u32[]{:S(2)}, u32[]{:S(2)}) %collective-permute-start.3) | collective-permute-done | bytes 393248 | tf_op jit(solution)/shard_map/ppermute | solution.py:44
  72.7 6.2 %collective-permute-done.2 = f32[3,1,8,4096]{3,2,1,0:T(8,128)S(1)} collective-permute-done((f32[3,1,8,4096]{3,2,1,0:T(8,128)S(1)}, f32[3,1,8,4096]{3,2,1,0:T(8,128)S(1)}, u32[]{:S(2)}, u32[]{:S(2)}) %collective-permute-start.2) | collective-permute-done | bytes 393248 | tf_op jit(solution)/shard_map/ppermute | solution.py:43
  79.0 1.1 pad_maximum_fusion
  80.0 0.9 reshape.198
  81.0 3.3 %gather_fusion.5 = f32[160,64,64]{2,1,0:T(8,128)} fusion(f32[72,64,64]{2,1,0:T(8,128)S(1)} %reshape.198, s32[1024]{0:T(1024)S(1)} %pad_clamp_fusion), kind=kCustom, calls=%fused_computation.5 | custom fusion | bytes 5243520 | tf_op jit(solution)/shard_map/jit(_take)/gather | solution.py:82
  84.3 11.1 %multiply_subtract_fusion = (f32[8,20,64,64]{3,2,1,0:T(8,128)}, f32[8,20,64,64]{3,2,1,0:T(8,128)}) fusion(f32[8,64]{1,0:T(8,128)S(1)} %copy.26, f32[8,64,64]{2,1,0:T(8,128)S(1)} %copy-done.6, pred[20]{0:T(512)(128)(4,1)S(1)} %copy-done.10, f32[8,20,64,64]{3,2,1,0:T(8,128)} %copy.27, f32[8,20,64,64]{3,2,1,0:T(8,128)} %bitcast.71, ...), kind=kOutput, calls=%fused_computation.6 | convolution fusion | flops 505937920 | bytes 10619060 | tf_op jit(solution)/shard_map/ksab,ksbc->ksac/dot_general | solution.py:85
  95.4 4.1 %reshape.261 = f32[8,20,4096]{2,1,0:T(8,128)S(1)} reshape(f32[8,20,64,64]{3,2,1,0:T(8,128)} %get-tuple-element.33) | data formatting | bytes 5242880 | tf_op jit(solution)/shard_map/reshape | solution.py:110
  99.5 1.3 fusion.12
  100.8 1.8 %copy.34 = f32[8,10,4096]{2,0,1:T(8,128)} copy(f32[8,10,4096]{2,1,0:T(8,128)S(1)} %fusion.12) | data formatting | bytes 2621440 | tf_op jit(solution)/shard_map/ksg,ksm->kgm/dot_general | solution.py:107
  102.6 2.2 %reshape.202 = f32[8,10,64,64]{3,2,0,1:T(8,128)S(1)} reshape(f32[8,10,4096]{2,0,1:T(8,128)} %copy.34) | data formatting | bytes 2621440 | tf_op jit(solution)/shard_map/reshape | solution.py:117
  104.8 2.1 %copy.35 = f32[8,64,10,64]{1,0,3,2:T(8,128)} copy(f32[8,64,10,64]{3,1,0,2:T(8,128)S(1)} %bitcast.73) | data formatting | bytes 2621440 | tf_op jit(solution)/shard_map/transpose | solution.py:116
  107.0 2.9 %reshape.203 = f32[512,640]{0,1:T(8,128)} reshape(f32[8,64,10,64]{1,0,3,2:T(8,128)} %copy.35) | data formatting | bytes 2621440 | tf_op jit(solution)/shard_map/reshape | solution.py:118
  109.9 3.8 %collective-permute-start.5 = (f32[512,640]{0,1:T(8,128)}, f32[512,640]{0,1:T(8,128)}, u32[]{:S(2)}, u32[]{:S(2)}) collective-permute-start(f32[512,640]{0,1:T(8,128)} %reshape.203), channel_id=1, source_target_pairs={{0,16},{16,32},{32,48},{48,64},{64,80},{80,96},{96,112},{1,17},{17... | collective-permute-start | bytes 3932168 | tf_op jit(solution)/shard_map/ppermute | solution.py:52
  113.7 1.9 %collective-permute-start.7 = (f32[512,640]{0,1:T(8,128)}, f32[512,640]{0,1:T(8,128)}, u32[]{:S(2)}, u32[]{:S(2)}) collective-permute-start(f32[512,640]{0,1:T(8,128)} %reshape.203), channel_id=1, source_target_pairs={{0,1},{1,2},{2,3},{3,4},{4,5},{5,6},{6,7},{7,8},{8,9},{9,10},{10,1... | collective-permute-start | bytes 3932168 | tf_op jit(solution)/shard_map/ppermute | solution.py:52
  115.6 5.5 %collective-permute-start.9 = (f32[512,640]{0,1:T(8,128)}, f32[512,640]{0,1:T(8,128)}, u32[]{:S(2)}, u32[]{:S(2)}) collective-permute-start(f32[512,640]{0,1:T(8,128)} %reshape.203), channel_id=1, source_target_pairs={{1,0},{2,1},{3,2},{4,3},{5,4},{6,5},{7,6},{8,7},{9,8},{10,9},{11,1... | collective-permute-start | bytes 3932168 | tf_op jit(solution)/shard_map/ppermute | solution.py:52
  121.1 2.3 %collective-permute-start.11 = (f32[512,640]{0,1:T(8,128)}, f32[512,640]{0,1:T(8,128)}, u32[]{:S(2)}, u32[]{:S(2)}) collective-permute-start(f32[512,640]{0,1:T(8,128)} %reshape.203), channel_id=1, source_target_pairs={{16,0},{32,16},{48,32},{64,48},{80,64},{96,80},{112,96},{17,1},{33... | collective-permute-start | bytes 3932168 | tf_op jit(solution)/shard_map/ppermute | solution.py:52
  123.4 4.1 %reshape.260 = f32[8,20,4096]{2,1,0:T(8,128)S(1)} reshape(f32[8,20,64,64]{3,2,1,0:T(8,128)} %get-tuple-element.32) | data formatting | bytes 5242880 | tf_op jit(solution)/shard_map/reshape | solution.py:104
  127.5 1.3 fusion.13
  128.8 1.8 %copy.30 = f32[8,10,4096]{2,0,1:T(8,128)} copy(f32[8,10,4096]{2,1,0:T(8,128)S(1)} %fusion.13) | data formatting | bytes 2621440 | tf_op jit(solution)/shard_map/ksg,ksm->kgm/dot_general | solution.py:101
  130.7 2.2 %reshape.200 = f32[8,5,2,64,64]{4,3,0,2,1:T(8,128)S(1)} reshape(f32[8,10,4096]{2,0,1:T(8,128)} %copy.30) | data formatting | bytes 2621440 | tf_op jit(solution)/shard_map/reshape | solution.py:114
  132.9 1.4 fusion.21
  134.3 1.3 copy.31
  135.8 3.4 %collective-permute-start.4 = (f32[512,128]{0,1:T(8,128)S(1)}, f32[512,128]{0,1:T(8,128)S(1)}, u32[]{:S(2)}, u32[]{:S(2)}) collective-permute-start(f32[512,128]{0,1:T(8,128)S(1)} %squeeze.13), channel_id=1, source_target_pairs={{0,16},{16,32},{32,48},{48,64},{64,80},{80,96},{96,112},{1,17},{17... | collective-permute-start | bytes 786440 | tf_op jit(solution)/shard_map/ppermute | solution.py:52
  139.2 1.3 copy.38
  141.8 2.7 %fusion.28 = f32[128,5,128]{2,0,1:T(8,128)S(1)} fusion(f32[512,128,1]{0,1,2:T(8,128)S(1)} %reshape.259, f32[5,128,512]{2,1,0:T(8,128)} %bitcast.13), kind=kOutput, calls=%fused_computation.82 | convolution fusion | flops 503316480 | bytes 1900544 | tf_op jit(solution)/shard_map/dot_general | solution.py:56
  144.5 1.9 %collective-permute-start.6 = (f32[512,128]{0,1:T(8,128)S(1)}, f32[512,128]{0,1:T(8,128)S(1)}, u32[]{:S(2)}, u32[]{:S(2)}) collective-permute-start(f32[512,128]{0,1:T(8,128)S(1)} %squeeze.14), channel_id=1, source_target_pairs={{0,1},{1,2},{2,3},{3,4},{4,5},{5,6},{6,7},{7,8},{8,9},{9,10},{10,1... | collective-permute-start | bytes 786440 | tf_op jit(solution)/shard_map/ppermute | solution.py:52
  146.5 5.5 %collective-permute-start.8 = (f32[512,128]{0,1:T(8,128)S(1)}, f32[512,128]{0,1:T(8,128)S(1)}, u32[]{:S(2)}, u32[]{:S(2)}) collective-permute-start(f32[512,128]{0,1:T(8,128)S(1)} %squeeze.16), channel_id=1, source_target_pairs={{1,0},{2,1},{3,2},{4,3},{5,4},{6,5},{7,6},{8,7},{9,8},{10,9},{11,1... | collective-permute-start | bytes 786440 | tf_op jit(solution)/shard_map/ppermute | solution.py:52
  152.0 2.5 %fusion.26 = f32[128,640]{0,1:T(8,128)S(1)} fusion(f32[512,128]{0,1:T(8,128)S(1)} %collective-permute-done.4, f32[512,640]{0,1:T(8,128)} %collective-permute-done.5), kind=kOutput, calls=%fused_computation.80 | convolution fusion | flops 503316480 | bytes 1900544 | tf_op jit(solution)/shard_map/dot_general | solution.py:56
  154.5 1.5 collective-permute-done.6
  156.0 2.4 %collective-permute-start.10 = (f32[512,128]{0,1:T(8,128)S(1)}, f32[512,128]{0,1:T(8,128)S(1)}, u32[]{:S(2)}, u32[]{:S(2)}) collective-permute-start(f32[512,128]{0,1:T(8,128)S(1)} %squeeze.17), channel_id=1, source_target_pairs={{16,0},{32,16},{48,32},{64,48},{80,64},{96,80},{112,96},{17,1},{33... | collective-permute-start | bytes 786440 | tf_op jit(solution)/shard_map/ppermute | solution.py:52
  158.4 2.5 %fusion.27 = f32[128,640]{0,1:T(8,128)S(1)} fusion(f32[512,128]{0,1:T(8,128)S(1)} %collective-permute-done.6, f32[512,640]{0,1:T(8,128)} %collective-permute-done.7), kind=kOutput, calls=%fused_computation.81 | convolution fusion | flops 503316480 | bytes 1900544 | tf_op jit(solution)/shard_map/dot_general | solution.py:56
  161.4 2.5 %fusion.29 = f32[128,640]{0,1:T(8,128)S(1)} fusion(f32[512,128]{0,1:T(8,128)S(1)} %collective-permute-done.8, f32[512,640]{0,1:T(8,128)} %collective-permute-done.9), kind=kOutput, calls=%fused_computation.83 | convolution fusion | flops 503316480 | bytes 1900544 | tf_op jit(solution)/shard_map/dot_general | solution.py:56
  164.5 2.5 %fusion.30 = f32[128,640]{0,1:T(8,128)S(1)} fusion(f32[512,128]{0,1:T(8,128)S(1)} %collective-permute-done.10, f32[512,640]{0,1:T(8,128)} %collective-permute-done.11), kind=kOutput, calls=%fused_computation.84 | convolution fusion | flops 503316480 | bytes 1900544 | tf_op jit(solution)/shard_map/dot_general | solution.py:56
  168.8 1.0 reshape.208
  (104 shorter events, 5.7 us)
Async XLA Ops:
  0.0 57.9 %copy-start = (s32[1024]{0:T(1024)S(1)}, s32[1024]{0:T(1024)}, u32[]{:S(2)}) copy-start(s32[1024]{0:T(1024)} %param.12) | copy-start | bytes 12292
  0.0 59.8 %collective-permute-start.1 = (f32[1,1,8,4096]{3,2,1,0:T(8,128)}, f32[1,1,8,4096]{3,2,1,0:T(8,128)S(1)}, u32[]{:S(2)}, u32[]{:S(2)}) collective-permute-start(f32[1,1,8,4096]{3,2,1,0:T(8,128)} %bitcast.78), channel_id=1, source_target_pairs={{16,0},{32,16},{48,32},{64,48},{80,64},{96,80},{112,96},{17,1},{33... | collective-permute-start | bytes 393224 | tf_op jit(solution)/shard_map/ppermute | solution.py:44
  2.7 57.1 %collective-permute-start = (f32[1,1,8,4096]{3,2,1,0:T(8,128)}, f32[1,1,8,4096]{3,2,1,0:T(8,128)S(1)}, u32[]{:S(2)}, u32[]{:S(2)}) collective-permute-start(f32[1,1,8,4096]{3,2,1,0:T(8,128)} %bitcast.79), channel_id=1, source_target_pairs={{0,16},{16,32},{32,48},{48,64},{64,80},{80,96},{96,112},{1,17},{17... | collective-permute-start | bytes 393224 | tf_op jit(solution)/shard_map/ppermute | solution.py:43
  29.2 2.7 %copy-start.2 = (s32[5]{0:T(128)S(1)}, s32[5]{0:T(128)}, u32[]{:S(2)}) copy-start(s32[5]{0:T(128)} %constant.128.clone) | copy-start | bytes 64
  29.2 3.4 %copy-start.11 = (s32[5]{0:T(128)S(1)}, s32[5]{0:T(128)}, u32[]{:S(2)}) copy-start(s32[5]{0:T(128)} %constant.127.clone) | copy-start | bytes 64
  29.2 3.4 %copy-start.12 = (s32[5]{0:T(128)S(1)}, s32[5]{0:T(128)}, u32[]{:S(2)}) copy-start(s32[5]{0:T(128)} %constant.126.clone) | copy-start | bytes 64
  29.2 4.2 %copy-start.9 = (s32[8,20]{1,0:T(8,128)S(1)}, s32[8,20]{1,0:T(8,128)}, u32[]{:S(2)}) copy-start(s32[8,20]{1,0:T(8,128)} %param.9) | copy-start | bytes 1924
  29.2 4.3 %copy-start.5 = (f32[8,4096]{1,0:T(8,128)S(1)}, f32[8,4096]{1,0:T(8,128)}, u32[]{:S(2)}) copy-start(f32[8,4096]{1,0:T(8,128)} %param.11) | copy-start | bytes 393220
  59.8 13.0 %copy-start.7 = (f32[1,1,8,4096]{3,2,1,0:T(8,128)}, f32[1,1,8,4096]{3,2,1,0:T(8,128)S(1)}, u32[]{:S(2)}) copy-start(f32[1,1,8,4096]{3,2,1,0:T(8,128)S(1)} %collective-permute-done.1) | copy-start | bytes 393220
  59.8 13.0 %copy-start.8 = (f32[1,1,8,4096]{3,2,1,0:T(8,128)}, f32[1,1,8,4096]{3,2,1,0:T(8,128)S(1)}, u32[]{:S(2)}) copy-start(f32[1,1,8,4096]{3,2,1,0:T(8,128)S(1)} %collective-permute-done) | copy-start | bytes 393220
  59.8 12.9 %collective-permute-start.3 = (f32[3,1,8,4096]{3,2,1,0:T(8,128)S(1)}, f32[3,1,8,4096]{3,2,1,0:T(8,128)S(1)}, u32[]{:S(2)}, u32[]{:S(2)}) collective-permute-start(f32[3,1,8,4096]{3,2,1,0:T(8,128)S(1)} %pad_maximum_fusion.1), channel_id=1, source_target_pairs={{1,0},{2,1},{3,2},{4,3},{5,4},{6,5},{7,6},{8,7},{9,8},{10,9},{11,1... | collective-permute-start | bytes 1179656 | tf_op jit(solution)/shard_map/ppermute | solution.py:44
  64.4 14.6 %collective-permute-start.2 = (f32[3,1,8,4096]{3,2,1,0:T(8,128)S(1)}, f32[3,1,8,4096]{3,2,1,0:T(8,128)S(1)}, u32[]{:S(2)}, u32[]{:S(2)}) collective-permute-start(f32[3,1,8,4096]{3,2,1,0:T(8,128)S(1)} %pad_maximum_fusion.1), channel_id=1, source_target_pairs={{0,1},{1,2},{2,3},{3,4},{4,5},{5,6},{6,7},{7,8},{8,9},{9,10},{10,1... | collective-permute-start | bytes 1179656 | tf_op jit(solution)/shard_map/ppermute | solution.py:43
  81.0 3.3 %copy-start.6 = (f32[8,64,64]{2,1,0:T(8,128)S(1)}, f32[8,64,64]{2,1,0:T(8,128)}, u32[]{:S(2)}) copy-start(f32[8,64,64]{2,1,0:T(8,128)} %broadcast_in_dim.80) | copy-start | bytes 393220
  81.0 3.3 %copy-start.10 = (pred[20]{0:T(512)(128)(4,1)S(1)}, pred[20]{0:T(512)(128)(4,1)}, u32[]{:S(2)}) copy-start(pred[20]{0:T(512)(128)(4,1)} %iota_compare_fusion.3) | copy-start | bytes 64
  109.9 36.6 %collective-permute-start.5 = (f32[512,640]{0,1:T(8,128)}, f32[512,640]{0,1:T(8,128)}, u32[]{:S(2)}, u32[]{:S(2)}) collective-permute-start(f32[512,640]{0,1:T(8,128)} %reshape.203), channel_id=1, source_target_pairs={{0,16},{16,32},{32,48},{48,64},{64,80},{80,96},{96,112},{1,17},{17... | collective-permute-start | bytes 3932168 | tf_op jit(solution)/shard_map/ppermute | solution.py:52
  113.7 44.7 %collective-permute-start.7 = (f32[512,640]{0,1:T(8,128)}, f32[512,640]{0,1:T(8,128)}, u32[]{:S(2)}, u32[]{:S(2)}) collective-permute-start(f32[512,640]{0,1:T(8,128)} %reshape.203), channel_id=1, source_target_pairs={{0,1},{1,2},{2,3},{3,4},{4,5},{5,6},{6,7},{7,8},{8,9},{9,10},{10,1... | collective-permute-start | bytes 3932168 | tf_op jit(solution)/shard_map/ppermute | solution.py:52
  115.6 45.8 %collective-permute-start.9 = (f32[512,640]{0,1:T(8,128)}, f32[512,640]{0,1:T(8,128)}, u32[]{:S(2)}, u32[]{:S(2)}) collective-permute-start(f32[512,640]{0,1:T(8,128)} %reshape.203), channel_id=1, source_target_pairs={{1,0},{2,1},{3,2},{4,3},{5,4},{6,5},{7,6},{8,7},{9,8},{10,9},{11,1... | collective-permute-start | bytes 3932168 | tf_op jit(solution)/shard_map/ppermute | solution.py:52
  121.1 43.4 %collective-permute-start.11 = (f32[512,640]{0,1:T(8,128)}, f32[512,640]{0,1:T(8,128)}, u32[]{:S(2)}, u32[]{:S(2)}) collective-permute-start(f32[512,640]{0,1:T(8,128)} %reshape.203), channel_id=1, source_target_pairs={{16,0},{32,16},{48,32},{64,48},{80,64},{96,80},{112,96},{17,1},{33... | collective-permute-start | bytes 3932168 | tf_op jit(solution)/shard_map/ppermute | solution.py:52
  134.3 6.4 %copy-start.4 = (f32[1,8,64,2,64]{4,2,1,3,0:T(8,128)S(1)}, f32[1,8,64,2,64]{4,2,1,3,0:T(8,128)}, u32[]{:S(2)}) copy-start(f32[1,8,64,2,64]{4,2,1,3,0:T(8,128)} %get-tuple-element.9) | copy-start | bytes 786436
  135.6 5.4 %copy-start.3 = (f32[1,8,64,2,64]{4,2,1,3,0:T(8,128)S(1)}, f32[1,8,64,2,64]{4,2,1,3,0:T(8,128)}, u32[]{:S(2)}) copy-start(f32[1,8,64,2,64]{4,2,1,3,0:T(8,128)} %get-tuple-element.8) | copy-start | bytes 786436
  135.8 8.7 %collective-permute-start.4 = (f32[512,128]{0,1:T(8,128)S(1)}, f32[512,128]{0,1:T(8,128)S(1)}, u32[]{:S(2)}, u32[]{:S(2)}) collective-permute-start(f32[512,128]{0,1:T(8,128)S(1)} %squeeze.13), channel_id=1, source_target_pairs={{0,16},{16,32},{32,48},{48,64},{64,80},{80,96},{96,112},{1,17},{17... | collective-permute-start | bytes 786440 | tf_op jit(solution)/shard_map/ppermute | solution.py:52
  144.5 11.5 %collective-permute-start.6 = (f32[512,128]{0,1:T(8,128)S(1)}, f32[512,128]{0,1:T(8,128)S(1)}, u32[]{:S(2)}, u32[]{:S(2)}) collective-permute-start(f32[512,128]{0,1:T(8,128)S(1)} %squeeze.14), channel_id=1, source_target_pairs={{0,1},{1,2},{2,3},{3,4},{4,5},{5,6},{6,7},{7,8},{8,9},{9,10},{10,1... | collective-permute-start | bytes 786440 | tf_op jit(solution)/shard_map/ppermute | solution.py:52
  146.5 14.9 %collective-permute-start.8 = (f32[512,128]{0,1:T(8,128)S(1)}, f32[512,128]{0,1:T(8,128)S(1)}, u32[]{:S(2)}, u32[]{:S(2)}) collective-permute-start(f32[512,128]{0,1:T(8,128)S(1)} %squeeze.16), channel_id=1, source_target_pairs={{1,0},{2,1},{3,2},{4,3},{5,4},{6,5},{7,6},{8,7},{9,8},{10,9},{11,1... | collective-permute-start | bytes 786440 | tf_op jit(solution)/shard_map/ppermute | solution.py:52
  156.0 8.4 %collective-permute-start.10 = (f32[512,128]{0,1:T(8,128)S(1)}, f32[512,128]{0,1:T(8,128)S(1)}, u32[]{:S(2)}, u32[]{:S(2)}) collective-permute-start(f32[512,128]{0,1:T(8,128)S(1)} %squeeze.17), channel_id=1, source_target_pairs={{16,0},{32,16},{48,32},{64,48},{80,64},{96,80},{112,96},{17,1},{33... | collective-permute-start | bytes 786440 | tf_op jit(solution)/shard_map/ppermute | solution.py:52
  168.2 1.7 copy-start.1
where the time goes:
time: 171 us; the launch traced here: 170 us
  local copies, waits for them, and re-layouts  85 us (50%)
  starting transfers between devices  39.6 us (23%)
  matrix products  26.5 us (15%)
  waiting for transfers between devices  14 us (8%)
  other arithmetic  4.04 us (2%)
    ppermute x8, starting transfers between devices, from_behind(): return lax.ppermute(x, axis, pairs)  26.7 us
    reshape x1, local copies, waits for them, and re-layouts, body(): jnp.where(live_mask[:, :, None], stiffness_blocks, 0.0)  23.5 us
    select_n x1, local copies, waits for them, and re-layouts, body(): jnp.where(live_mask[:, :, None], stiffness_blocks, 0.0)  19.5 us
    dot_general x5, matrix products, coarse_rows(): lax.dot_general(left_side, right_side, (((0,), (0,)), ((), ())), precisio...  12.7 us
    dot_general x1, matrix products, body(): jnp.einsum('ksab,ksbc->ksac', blocks, picked, precision=HIGHEST)  11.1 us
    ppermute x2, starting transfers between devices, padded(): after = lax.ppermute(leading, axis, down)  7.27 us
    ppermute x2, waiting for transfers between devices, padded(): before = lax.ppermute(last, axis, up)  6.22 us
    ppermute x2, waiting for transfers between devices, padded(): after = lax.ppermute(leading, axis, down)  6.2 us
  transfers between devices with their start and end apart: 12, of which 3 were waited for; matrix products, arithmetic and copies ran while one was open for 47% of the time, Pallas kernels for 0%

commit v1 on v0

v1 whole, which is shorter than its diff:
```python
import jax
import jax.numpy as jnp
from jax import lax
from jax.experimental import pallas as pl
from jax.experimental.pallas import tpu as pltpu
from jax.sharding import PartitionSpec as P

MESH = pl.DeviceIdType.MESH
F32 = jnp.float32
BF16 = jnp.bfloat16

FINE = 64
BLOCKS = 8
SLOTS = 20
ROW_SLOTS = 4
CHUNKS = 32
LANES = 128
OMEGA = 2.0 / 3.0

STEPS = ((0, 0), (-1, 0), (1, 0), (0, -1), (0, 1))
CLASS = (0, 3, 4, 1, 2)
OPPOSITE = (0, 2, 1, 4, 3)
BAND_STEPS = (
    (-2, 0),
    (-1, -1),
    (-1, 0),
    (-1, 1),
    (0, -2),
    (0, -1),
    (0, 0),
    (0, 1),
    (0, 2),
    (1, -1),
    (1, 0),
    (1, 1),
    (2, 0),
)
OFFSETS = 13
NEAR = 5


def band_of(source, target):
    a, b = STEPS[source], STEPS[target]
    return BAND_STEPS.index((a[0] + b[0], a[1] + b[1]))


def dot(a, b):
    return jnp.dot(a, b, preferred_element_type=F32)


def split(x):
    high = x.astype(BF16)
    return high, (x - high.astype(F32)).astype(BF16)


def kernel(
    rows,
    cols,
    stiff,
    columns,
    counts,
    tiles,
    aggs,
    out,
    xbuf,
    compact,
    dense,
    tp,
    tpack,
    weights,
    damp,
    right,
    left,
    gsend,
    grecv,
    acc,
    xsem,
    tsem,
    osem,
    tsend,
    trecv,
    gsend_sem,
    grecv_sem,
):
    my_row = lax.axis_index("row")
    my_col = lax.axis_index("col")
    places = [
        (lax.rem(my_row + s[0] + rows, rows), lax.rem(my_col + s[1] + cols, cols)) for s in STEPS
    ]

    barrier = pltpu.get_barrier_semaphore()
    for q in range(1, NEAR):
        pl.semaphore_signal(barrier, inc=1, device_id=places[q], device_id_type=MESH)

    for i in range(CHUNKS):
        pltpu.make_async_copy(tiles.at[:, pl.ds(i * LANES, LANES)], tp.at[:, i, :], tsem).start()
    for i in range(CHUNKS):
        pltpu.make_async_copy(
            stiff.at[:, :, pl.ds(i * LANES, LANES)], xbuf.at[:, :, i, :], xsem
        ).start()

    lane = lax.broadcasted_iota(jnp.int32, (1, LANES), 1)
    low_half = lane < FINE
    half = jnp.where(low_half, 0, 1)

    pltpu.make_async_copy(tp, tp, tsem).wait()
    for pair in range(BLOCKS // 2):
        a, b = tp[2 * pair], tp[2 * pair + 1]
        tpack[0, pair, pl.ds(0, CHUNKS, 2), :] = jnp.where(low_half, a, pltpu.roll(b, FINE, 1))
        tpack[0, pair, pl.ds(1, CHUNKS, 2), :] = jnp.where(low_half, pltpu.roll(a, FINE, 1), b)

    pl.semaphore_wait(barrier, NEAR - 1)

    def tile_copy(q):
        return pltpu.make_async_remote_copy(
            src_ref=tpack.at[0],
            dst_ref=tpack.at[OPPOSITE[q]],
            send_sem=tsend.at[q],
            recv_sem=trecv.at[OPPOSITE[q]],
            device_id=places[q],
            device_id_type=MESH,
        )

    def arrival(q):
        return pltpu.make_async_remote_copy(
            src_ref=tpack.at[0],
            dst_ref=tpack.at[q],
            send_sem=tsend.at[q],
            recv_sem=trecv.at[q],
            device_id=places[q],
            device_id_type=MESH,
        )

    for q in (3, 4, 1, 2):
        tile_copy(q).start()

    weights[...] = jnp.zeros_like(weights)
    zero = jnp.zeros((CHUNKS, LANES), BF16)

    pltpu.make_async_copy(xbuf, xbuf, xsem).wait()

    row_at = lax.broadcasted_iota(jnp.int32, (CHUNKS, LANES), 0)
    lane_at = lax.broadcasted_iota(jnp.int32, (CHUNKS, LANES), 1)

    def spread(k, _):
        rows_k = pl.ds(pl.multiple_of(k * CHUNKS, CHUNKS), CHUNKS)
        x0 = xbuf[0, k]
        for p in range(2):
            diagonal = jnp.sum(
                jnp.where(lane_at == 2 * row_at + p * (FINE + 1), x0, 0.0), axis=1, keepdims=True
            )
            damp[p, rows_k, :] = jnp.broadcast_to(OMEGA / diagonal, (CHUNKS, LANES))
        for q in range(NEAR):
            compact[0, q, 0] = zero
            compact[1, q, 0] = zero
            count = counts[k, CLASS[q]]
            word = jnp.int32(0)
            for t in range(ROW_SLOTS):
                slot = CLASS[q] * ROW_SLOTS + t
                high, low = split(xbuf[slot, k])
                compact[0, q, t + 1] = high
                compact[1, q, t + 1] = low
                word = word | jnp.where(t < count, (t + 1) << (columns[k, slot] * 4), 0)
            for j in range(BLOCKS):
                e = (word >> (4 * j)) & 7
                lanes_j = slice(j * LANES, (j + 1) * LANES)
                dense[q, 0, rows_k, lanes_j] = compact[0, q, e]
                dense[q, 1, rows_k, lanes_j] = compact[1, q, e]
        return 0

    lax.fori_loop(0, BLOCKS, spread, 0)

    def near_aggs(q):
        first = (places[q][0] * cols + places[q][1]) * BLOCKS
        return [aggs[first + j] & 1 for j in range(BLOCKS)]

    def smooth(q):
        groups = near_aggs(q)
        for pair in range(BLOCKS // 2):
            v = tpack[q, pair]
            r = pltpu.roll(v, FINE, 1)
            both = (jnp.where(low_half, v, r), jnp.where(low_half, r, v))
            for side in range(2):
                j = 2 * pair + side
                high, low = split(jnp.where(half == groups[j], both[side], 0.0))
                for p in range(2):
                    rows_j = slice(j * LANES + p * FINE, j * LANES + (p + 1) * FINE)
                    weights[0, rows_j, p * LANES : (p + 1) * LANES] = high
                    weights[1, rows_j, p * LANES : (p + 1) * LANES] = low
        s = (
            dot(dense[q, 0], weights[0])
            + dot(dense[q, 1], weights[0])
            + dot(dense[q, 0], weights[1])
        )
        for p in range(2):
            s_p = s[:, p * LANES : (p + 1) * LANES]
            rows_p = slice(p * 256, (p + 1) * 256)
            high, low = split(s_p)
            right[0, rows_p, q * LANES : (q + 1) * LANES] = high
            right[1, rows_p, q * LANES : (q + 1) * LANES] = low
            l_p = -(damp[p] * s_p)
            if q == 0:
                own = []
                for k in range(BLOCKS):
                    t_k = tp[k]
                    r_k = pltpu.roll(t_k, FINE, 1)
                    t_both = jnp.where(low_half, t_k, r_k) if p == 0 else jnp.where(low_half, r_k, t_k)
                    own.append(jnp.where(half == groups[k], t_both, 0.0))
                l_p = l_p + jnp.concatenate(own, axis=0)
            high, low = split(l_p.T)
            left[0, q * LANES : (q + 1) * LANES, rows_p] = high
            left[1, q * LANES : (q + 1) * LANES, rows_p] = low

    def products(q_from, q_to, m_from, m_to):
        rows_l = slice(q_from * LANES, q_to * LANES)
        cols_r = slice(m_from * LANES, m_to * LANES)
        return (
            dot(left[0, rows_l, :], right[0, :, cols_r])
            + dot(left[1, rows_l, :], right[0, :, cols_r])
            + dot(left[0, rows_l, :], right[1, :, cols_r])
        )

    def piece_copy(q, m):
        return pltpu.make_async_remote_copy(
            src_ref=gsend.at[q, m],
            dst_ref=grecv.at[OPPOSITE[q], m],
            send_sem=gsend_sem.at[q, m],
            recv_sem=grecv_sem.at[OPPOSITE[q], m],
            device_id=places[q],
            device_id_type=MESH,
        )

    def piece_arrival(q, m):
        return pltpu.make_async_remote_copy(
            src_ref=gsend.at[q, m],
            dst_ref=grecv.at[q, m],
            send_sem=gsend_sem.at[q, m],
            recv_sem=grecv_sem.at[q, m],
            device_id=places[q],
            device_id_type=MESH,
        )

    def make_and_send(q_from, q_to, m_from, m_to):
        g = products(q_from, q_to, m_from, m_to)
        for m in range(m_from, m_to):
            for q in range(q_from, q_to):
                part = g[
                    (q - q_from) * LANES : (q - q_from + 1) * LANES,
                    (m - m_from) * LANES : (m - m_from + 1) * LANES,
                ]
                gsend[q, m] = part
                piece_copy(q, m).start()

    smooth(0)
    for q in (1, 2, 3, 4):
        arrival(q).wait_recv()
        smooth(q)
    for m_from, m_to in ((0, 2), (2, 4), (4, 5)):
        make_and_send(3, 5, m_from, m_to)
    for m_from, m_to in ((0, 2), (2, 4), (4, 5)):
        make_and_send(1, 3, m_from, m_to)
    own_products = products(0, 1, 0, NEAR)
    for m in range(NEAR):
        acc[band_of(0, m)] = own_products[:, m * LANES : (m + 1) * LANES]
    started = {band_of(0, m) for m in range(NEAR)}
    for m in range(NEAR):
        for q in (1, 2, 3, 4):
            piece_arrival(q, m).wait_recv()
            o = band_of(q, m)
            if o in started:
                acc[o] += grecv[q, m]
            else:
                acc[o] = grecv[q, m]
                started.add(o)

    def out_copy(o):
        return pltpu.make_async_copy(
            acc.at[o], out.at[:, pl.ds(o * LANES, LANES)], osem.at[o]
        )

    for o in range(OFFSETS):
        out_copy(o).start()
    for o in range(OFFSETS):
        out_copy(o).wait()
    for q in range(1, NEAR):
        tile_copy(q).wait_send()
        for m in range(NEAR):
            piece_copy(q, m).wait_send()


def solution(mesh):
    rows, cols = mesh.shape["row"], mesh.shape["col"]

    def body(stiffness_blocks, block_columns, block_counts, tentative_tiles, aggregate_of):
        any_spec = pl.BlockSpec(memory_space=pl.ANY)
        smem_spec = pl.BlockSpec(memory_space=pltpu.SMEM)
        dma = pltpu.SemaphoreType.DMA
        result = pl.pallas_call(
            lambda *refs: kernel(rows, cols, *refs),
            out_shape=jax.ShapeDtypeStruct((2 * FINE, OFFSETS * LANES), F32),
            in_specs=[any_spec, smem_spec, smem_spec, any_spec, smem_spec],
            out_specs=any_spec,
            scratch_shapes=[
                pltpu.VMEM((SLOTS, BLOCKS, CHUNKS, LANES), F32),
                pltpu.VMEM((2, NEAR, ROW_SLOTS + 1, CHUNKS, LANES), BF16),
                pltpu.VMEM((NEAR, 2, BLOCKS * CHUNKS, BLOCKS * LANES), BF16),
                pltpu.VMEM((BLOCKS, CHUNKS, LANES), F32),
                pltpu.VMEM((NEAR, BLOCKS // 2, FINE, LANES), F32),
                pltpu.VMEM((2, BLOCKS * LANES, 2 * LANES), BF16),
                pltpu.VMEM((2, BLOCKS * CHUNKS, LANES), F32),
                pltpu.VMEM((2, BLOCKS * FINE, NEAR * LANES), BF16),
                pltpu.VMEM((2, NEAR * LANES, BLOCKS * FINE), BF16),
                pltpu.VMEM((NEAR, NEAR, LANES, LANES), F32),
                pltpu.VMEM((NEAR, NEAR, LANES, LANES), F32),
                pltpu.VMEM((OFFSETS, LANES, LANES), F32),
                dma,
                dma,
                dma((OFFSETS,)),
                dma((NEAR,)),
                dma((NEAR,)),
                dma((NEAR, NEAR)),
                dma((NEAR, NEAR)),
            ],
            compiler_params=pltpu.CompilerParams(
                collective_id=0, has_side_effects=True, vmem_limit_bytes=56 << 20
            ),
        )(
            jnp.transpose(stiffness_blocks, (1, 0, 2)),
            block_columns,
            block_counts,
            tentative_tiles,
            aggregate_of,
        )
        return result.reshape(2, FINE, OFFSETS * LANES)

    by_device = P(("row", "col"), None)
    by_device3 = P(("row", "col"), None, None)
    return jax.shard_map(
        body,
        mesh=mesh,
        in_specs=(by_device3, by_device, by_device, by_device, P()),
        out_specs=by_device3,
        check_vma=False,
    )
```

time: 171 us -> 27.9 us (0.16)
  the two profiles are of different devices: /device:TPU:25 before, /device:TPU:0 now
where the time goes in v1:
time: 27.9 us; the launch traced here: 27.7 us
  Pallas kernels  25.6 us (92%)
  local copies, waits for them, and re-layouts  2.11 us (8%)
    pallas_call x1, Pallas kernels, body(): pl.pallas_call(lambda *refs: kernel(rows, cols, *refs), out_shape=jax.Sha...  25.6 us
    unnamed x1, local copies, waits for them, and re-layouts  2.11 us

profile of v1, /device:TPU:0, one launch (start us, length us, event | category | flops | bytes accessed | tf_op | source)
XLA Modules:
  0.0 27.7 jit_solution(9937379008843705756)
XLA Ops:
  0.0 25.6 %shard_map.55 = f32[128,1664]{1,0:T(8,128)} custom-call(f32[20,8,4096]{2,1,0:T(8,128)} %bitcast.3, s32[8,20]{1,0:T(8,128)} %refs_1_.1, s32[8,5]{1,0:T(8,128)} %refs_2_.1, f32[8,4096]{1,0:T(8,128)} %refs_3_.1, s32[1024]{0:T(1024)} %refs_4_.1), custom_call_target="tpu_custom_call" | custom-call | tf_op jit(solution)/shard_map/pallas_call | solution.py:298
  25.6 2.1 %copy.7 = f32[2,64,1664]{2,1,0:T(8,128)} copy(f32[2,64,1664]{2,1,0:T(8,128)} %bitcast.2) | data formatting | bytes 1703936

commit v2 on v1

--- a/solution.py
+++ b/solution.py
@@ -57,11 +57,14 @@
     rows,
     cols,
     stiff,
+    columns_in,
+    counts_in,
+    tiles,
+    aggs_in,
+    out,
     columns,
     counts,
-    tiles,
     aggs,
-    out,
     xbuf,
     compact,
     dense,
@@ -73,10 +76,9 @@
     left,
     gsend,
     grecv,
-    acc,
     xsem,
     tsem,
-    osem,
+    ssem,
     tsend,
     trecv,
     gsend_sem,
@@ -84,16 +86,33 @@
 ):
     my_row = lax.axis_index("row")
     my_col = lax.axis_index("col")
-    places = [
-        (lax.rem(my_row + s[0] + rows, rows), lax.rem(my_col + s[1] + cols, cols)) for s in STEPS
+    places = [(my_row + s[0], my_col + s[1]) for s in STEPS]
+    exists = [
+        None,
+        my_row > 0,
+        my_row < rows - 1,
+        my_col > 0,
+        my_col < cols - 1,
     ]
 
     barrier = pltpu.get_barrier_semaphore()
+    near_count = jnp.int32(0)
     for q in range(1, NEAR):
-        pl.semaphore_signal(barrier, inc=1, device_id=places[q], device_id_type=MESH)
+        near_count = near_count + jnp.where(exists[q], 1, 0)
+
+        @pl.when(exists[q])
+        def _():
+            pl.semaphore_signal(barrier, inc=1, device_id=places[q], device_id_type=MESH)
 
     for i in range(CHUNKS):
         pltpu.make_async_copy(tiles.at[:, pl.ds(i * LANES, LANES)], tp.at[:, i, :], tsem).start()
+    small = [
+        pltpu.make_async_copy(columns_in, columns, ssem.at[0]),
+        pltpu.make_async_copy(counts_in, counts, ssem.at[1]),
+        pltpu.make_async_copy(aggs_in, aggs, ssem.at[2]),
+    ]
+    for copy in small:
+        copy.start()
     for i in range(CHUNKS):
         pltpu.make_async_copy(
             stiff.at[:, :, pl.ds(i * LANES, LANES)], xbuf.at[:, :, i, :], xsem
@@ -109,7 +128,7 @@
         tpack[0, pair, pl.ds(0, CHUNKS, 2), :] = jnp.where(low_half, a, pltpu.roll(b, FINE, 1))
         tpack[0, pair, pl.ds(1, CHUNKS, 2), :] = jnp.where(low_half, pltpu.roll(a, FINE, 1), b)
 
-    pl.semaphore_wait(barrier, NEAR - 1)
+    pl.semaphore_wait(barrier, near_count)
 
     def tile_copy(q):
         return pltpu.make_async_remote_copy(
@@ -132,11 +151,25 @@
         )
 
     for q in (3, 4, 1, 2):
-        tile_copy(q).start()
+
+        @pl.when(exists[q])
+        def _():
+            tile_copy(q).start()
+
+        @pl.when(jnp.logical_not(exists[q]))
+        def _():
+            tpack[q] = jnp.zeros((BLOCKS // 2, FINE, LANES), F32)
+
+    own_bands = [band_of(0, m) for m in range(NEAR)]
+    for o in range(OFFSETS):
+        if o not in own_bands:
+            out[:, o * LANES : (o + 1) * LANES] = jnp.zeros((LANES, LANES), F32)
 
     weights[...] = jnp.zeros_like(weights)
     zero = jnp.zeros((CHUNKS, LANES), BF16)
 
+    for copy in small:
+        copy.wait()
     pltpu.make_async_copy(xbuf, xbuf, xsem).wait()
 
     row_at = lax.broadcasted_iota(jnp.int32, (CHUNKS, LANES), 0)
@@ -171,7 +204,9 @@
     lax.fori_loop(0, BLOCKS, spread, 0)
 
     def near_aggs(q):
-        first = (places[q][0] * cols + places[q][1]) * BLOCKS
+        near_row = jnp.clip(places[q][0], 0, rows - 1)
+        near_col = jnp.clip(places[q][1], 0, cols - 1)
+        first = (near_row * cols + near_col) * BLOCKS
         return [aggs[first + j] & 1 for j in range(BLOCKS)]
 
     def smooth(q):
@@ -242,50 +277,63 @@
 
     def make_and_send(q_from, q_to, m_from, m_to):
         g = products(q_from, q_to, m_from, m_to)
-        for m in range(m_from, m_to):
-            for q in range(q_from, q_to):
+        for q in range(q_from, q_to):
+            for m in range(m_from, m_to):
                 part = g[
                     (q - q_from) * LANES : (q - q_from + 1) * LANES,
                     (m - m_from) * LANES : (m - m_from + 1) * LANES,
                 ]
-                gsend[q, m] = part
-                piece_copy(q, m).start()
+                if q == 0:
+                    o = own_bands[m]
+                    out[:, o * LANES : (o + 1) * LANES] = part
+                else:
+                    gsend[q, m] = part
+        for q in range(max(q_from, 1), q_to):
+
+            @pl.when(exists[q])
+            def _():
+                for m in range(m_from, m_to):
+                    piece_copy(q, m).start()
+
+    def wait_tiles(q):
+        @pl.when(exists[q])
+        def _():
+            arrival(q).wait_recv()
 
     smooth(0)
-    for q in (1, 2, 3, 4):
-        arrival(q).wait_recv()
-        smooth(q)
-    for m_from, m_to in ((0, 2), (2, 4), (4, 5)):
-        make_and_send(3, 5, m_from, m_to)
-    for m_from, m_to in ((0, 2), (2, 4), (4, 5)):
-        make_and_send(1, 3, m_from, m_to)
-    own_products = products(0, 1, 0, NEAR)
-    for m in range(NEAR):
-        acc[band_of(0, m)] = own_products[:, m * LANES : (m + 1) * LANES]
-    started = {band_of(0, m) for m in range(NEAR)}
-    for m in range(NEAR):
-        for q in (1, 2, 3, 4):
-            piece_arrival(q, m).wait_recv()
-            o = band_of(q, m)
-            if o in started:
-                acc[o] += grecv[q, m]
-            else:
-                acc[o] = grecv[q, m]
-                started.add(o)
-
-    def out_copy(o):
-        return pltpu.make_async_copy(
-            acc.at[o], out.at[:, pl.ds(o * LANES, LANES)], osem.at[o]
-        )
-
-    for o in range(OFFSETS):
-        out_copy(o).start()
-    for o in range(OFFSETS):
-        out_copy(o).wait()
+    wait_tiles(1)
+    smooth(1)
+    wait_tiles(2)
+    smooth(2)
+    make_and_send(1, 3, 0, 2)
+    make_and_send(1, 3, 2, 3)
+    make_and_send(0, 1, 0, 3)
+    wait_tiles(3)
+    smooth(3)
+    wait_tiles(4)
+    smooth(4)
+    make_and_send(3, 5, 0, 2)
+    make_and_send(3, 5, 2, 4)
+    make_and_send(3, 5, 4, 5)
+    make_and_send(1, 3, 3, 5)
+    make_and_send(0, 1, 3, 5)
+    for q_group, m_group in (((1, 2), range(0, 3)), ((3, 4), range(0, 3)), ((1, 2), range(3, 5)), ((3, 4), range(3, 5))):
+        for m in m_group:
+            for q in q_group:
+
+                @pl.when(exists[q])
+                def _():
+                    piece_arrival(q, m).wait_recv()
+                    o = band_of(q, m)
+                    out[:, o * LANES : (o + 1) * LANES] += grecv[q, m]
+
     for q in range(1, NEAR):
-        tile_copy(q).wait_send()
-        for m in range(NEAR):
-            piece_copy(q, m).wait_send()
+
+        @pl.when(exists[q])
+        def _():
+            tile_copy(q).wait_send()
+            for m in range(NEAR):
+                piece_copy(q, m).wait_send()
 
 
 def solution(mesh):
@@ -293,14 +341,17 @@
 
     def body(stiffness_blocks, block_columns, block_counts, tentative_tiles, aggregate_of):
         any_spec = pl.BlockSpec(memory_space=pl.ANY)
-        smem_spec = pl.BlockSpec(memory_space=pltpu.SMEM)
+        in_hbm = lambda x: pltpu.with_memory_space_constraint(x, pltpu.HBM)
         dma = pltpu.SemaphoreType.DMA
         result = pl.pallas_call(
             lambda *refs: kernel(rows, cols, *refs),
             out_shape=jax.ShapeDtypeStruct((2 * FINE, OFFSETS * LANES), F32),
-            in_specs=[any_spec, smem_spec, smem_spec, any_spec, smem_spec],
-            out_specs=any_spec,
+            in_specs=[any_spec] * 5,
+            out_specs=pl.BlockSpec(memory_space=pltpu.VMEM),
             scratch_shapes=[
+                pltpu.SMEM((BLOCKS, SLOTS), jnp.int32),
+                pltpu.SMEM((BLOCKS, NEAR), jnp.int32),
+                pltpu.SMEM(aggregate_of.shape, jnp.int32),
                 pltpu.VMEM((SLOTS, BLOCKS, CHUNKS, LANES), F32),
                 pltpu.VMEM((2, NEAR, ROW_SLOTS + 1, CHUNKS, LANES), BF16),
                 pltpu.VMEM((NEAR, 2, BLOCKS * CHUNKS, BLOCKS * LANES), BF16),
@@ -312,24 +363,23 @@
                 pltpu.VMEM((2, NEAR * LANES, BLOCKS * FINE), BF16),
                 pltpu.VMEM((NEAR, NEAR, LANES, LANES), F32),
                 pltpu.VMEM((NEAR, NEAR, LANES, LANES), F32),
-                pltpu.VMEM((OFFSETS, LANES, LANES), F32),
                 dma,
                 dma,
-                dma((OFFSETS,)),
+                dma((3,)),
                 dma((NEAR,)),
                 dma((NEAR,)),
                 dma((NEAR, NEAR)),
                 dma((NEAR, NEAR)),
             ],
             compiler_params=pltpu.CompilerParams(
-                collective_id=0, has_side_effects=True, vmem_limit_bytes=56 << 20
+                collective_id=0, has_side_effects=True, vmem_limit_bytes=40 << 20
             ),
         )(
-            jnp.transpose(stiffness_blocks, (1, 0, 2)),
-            block_columns,
-            block_counts,
-            tentative_tiles,
-            aggregate_of,
+            in_hbm(jnp.transpose(stiffness_blocks, (1, 0, 2))),
+            in_hbm(block_columns),
+            in_hbm(block_counts),
+            in_hbm(tentative_tiles),
+            in_hbm(aggregate_of),
         )
         return result.reshape(2, FINE, OFFSETS * LANES)
 

time: 27.9 us -> 24.2 us (0.87)
  the two profiles are of different devices: /device:TPU:0 before, /device:TPU:25 now
where the time goes in v2:
time: 24.2 us; the launch traced here: 23.8 us
  Pallas kernels  22.9 us (95%)
  local copies, waits for them, and re-layouts  0.9 us (4%)
    pallas_call x1, Pallas kernels, body(): pl.pallas_call(lambda *refs: kernel(rows, cols, *refs), out_shape=jax.Sha...  22.9 us
    unnamed x1, local copies, waits for them, and re-layouts  0.9 us

profile of v2, /device:TPU:25, one launch (start us, length us, event | category | flops | bytes accessed | tf_op | source)
XLA Modules:
  0.0 23.8 jit_solution(10884312720624465134)
XLA Ops:
  0.0 22.9 %shard_map.55 = f32[128,1664]{1,0:T(8,128)S(1)} custom-call(f32[20,8,4096]{2,1,0:T(8,128)} %bitcast.3, s32[8,20]{1,0:T(8,128)} %refs_1_.1, s32[8,5]{1,0:T(8,128)} %refs_2_.1, f32[8,4096]{1,0:T(8,128)} %refs_3_.1, s32[1024]{0:T(1024)} %refs_4_.1), custom_call_target="tpu_custom_call" | custom-call | tf_op jit(solution)/shard_map/pallas_call | solution.py:346
  22.9 0.9 %copy.7 = f32[2,64,1664]{2,1,0:T(8,128)} copy(f32[2,64,1664]{2,1,0:T(8,128)S(1)} %bitcast.2) | data formatting | bytes 1703936

commit v3 on v2

--- a/solution.py
+++ b/solution.py
@@ -68,9 +68,11 @@
     xbuf,
     compact,
     dense,
+    order,
     tp,
     tpack,
     weights,
+    halves,
     damp,
     right,
     left,
@@ -113,69 +115,91 @@
     ]
     for copy in small:
         copy.start()
-    for i in range(CHUNKS):
-        pltpu.make_async_copy(
-            stiff.at[:, :, pl.ds(i * LANES, LANES)], xbuf.at[:, :, i, :], xsem
-        ).start()
+    for first, last, sem in ((0, ROW_SLOTS, xsem.at[0]), (ROW_SLOTS, SLOTS, xsem.at[1])):
+        for i in range(CHUNKS):
+            pltpu.make_async_copy(
+                stiff.at[first:last, :, pl.ds(i * LANES, LANES)], xbuf.at[first:last, :, i, :], sem
+            ).start()
 
     lane = lax.broadcasted_iota(jnp.int32, (1, LANES), 1)
     low_half = lane < FINE
     half = jnp.where(low_half, 0, 1)
 
+    for copy in small:
+        copy.wait()
+    own_groups = None
+    for q in range(NEAR):
+        near_row = jnp.clip(places[q][0], 0, rows - 1)
+        near_col = jnp.clip(places[q][1], 0, cols - 1)
+        first = (near_row * cols + near_col) * BLOCKS
+        groups = [aggs[first + j] & 1 for j in range(BLOCKS)]
+        word = jnp.int32(0)
+        ones = jnp.int32(0)
+        for j in range(BLOCKS):
+            at = jnp.where(groups[j] == 1, 4 + ones, j - ones)
+            word = word | (jnp.int32(j) << (4 * at))
+            ones = ones + groups[j]
+        if q == 0:
+            own_groups = groups
+        for n in range(BLOCKS):
+            order[q, n] = (word >> (4 * n)) & 7
+
     pltpu.make_async_copy(tp, tp, tsem).wait()
-    for pair in range(BLOCKS // 2):
-        a, b = tp[2 * pair], tp[2 * pair + 1]
-        tpack[0, pair, pl.ds(0, CHUNKS, 2), :] = jnp.where(low_half, a, pltpu.roll(b, FINE, 1))
-        tpack[0, pair, pl.ds(1, CHUNKS, 2), :] = jnp.where(low_half, pltpu.roll(a, FINE, 1), b)
-
-    pl.semaphore_wait(barrier, near_count)
-
-    def tile_copy(q):
+    for group in range(2):
+        for pair in range(2):
+            a = tp[order[0, 4 * group + 2 * pair]]
+            b = tp[order[0, 4 * group + 2 * pair + 1]]
+            tpack[0, group, pair, pl.ds(0, CHUNKS, 2), :] = jnp.where(low_half, a, pltpu.roll(b, FINE, 1))
+            tpack[0, group, pair, pl.ds(1, CHUNKS, 2), :] = jnp.where(low_half, pltpu.roll(a, FINE, 1), b)
+
+    def tile_copy(q, group):
         return pltpu.make_async_remote_copy(
-            src_ref=tpack.at[0],
-            dst_ref=tpack.at[OPPOSITE[q]],
-            send_sem=tsend.at[q],
-            recv_sem=trecv.at[OPPOSITE[q]],
+            src_ref=tpack.at[0, group],
+            dst_ref=tpack.at[OPPOSITE[q], group],
+            send_sem=tsend.at[q, group],
+            recv_sem=trecv.at[OPPOSITE[q], group],
             device_id=places[q],
             device_id_type=MESH,
         )
 
-    def arrival(q):
+    def arrival(q, group):
         return pltpu.make_async_remote_copy(
-            src_ref=tpack.at[0],
-            dst_ref=tpack.at[q],
-            send_sem=tsend.at[q],
-            recv_sem=trecv.at[q],
+            src_ref=tpack.at[0, group],
+            dst_ref=tpack.at[q, group],
+            send_sem=tsend.at[q, group],
+            recv_sem=trecv.at[q, group],
             device_id=places[q],
             device_id_type=MESH,
         )
 
-    for q in (3, 4, 1, 2):
-
-        @pl.when(exists[q])
-        def _():
-            tile_copy(q).start()
-
-        @pl.when(jnp.logical_not(exists[q]))
-        def _():
-            tpack[q] = jnp.zeros((BLOCKS // 2, FINE, LANES), F32)
-
     own_bands = [band_of(0, m) for m in range(NEAR)]
-    for o in range(OFFSETS):
-        if o not in own_bands:
-            out[:, o * LANES : (o + 1) * LANES] = jnp.zeros((LANES, LANES), F32)
-
-    weights[...] = jnp.zeros_like(weights)
-    zero = jnp.zeros((CHUNKS, LANES), BF16)
-
-    for copy in small:
-        copy.wait()
-    pltpu.make_async_copy(xbuf, xbuf, xsem).wait()
 
     row_at = lax.broadcasted_iota(jnp.int32, (CHUNKS, LANES), 0)
     lane_at = lax.broadcasted_iota(jnp.int32, (CHUNKS, LANES), 1)
 
-    def spread(k, _):
+    zero = jnp.zeros((CHUNKS, LANES), BF16)
+    for q in range(NEAR):
+        compact[q, 0, 0] = zero
+        compact[q, 1, 0] = zero
+
+    def spread(q, slots, k):
+        rows_k = pl.ds(pl.multiple_of(k * CHUNKS, CHUNKS), CHUNKS)
+        rows_low = pl.ds(pl.multiple_of(k * CHUNKS + 256, CHUNKS), CHUNKS)
+        count = counts[k, slots // ROW_SLOTS]
+        word = jnp.int32(0)
+        for t in range(ROW_SLOTS):
+            high, low = split(xbuf[slots + t, k])
+            compact[q, 0, t + 1] = high
+            compact[q, 1, t + 1] = low
+            word = word | jnp.where(t < count, (t + 1) << (columns[k, slots + t] * 4), 0)
+        for group in range(2):
+            for n in range(4):
+                e = (word >> (4 * order[q, 4 * group + n])) & 7
+                lanes_n = slice(n * LANES, (n + 1) * LANES)
+                dense[q, group, rows_k, lanes_n] = compact[q, 0, e]
+                dense[q, group, rows_low, lanes_n] = compact[q, 1, e]
+
+    def spread_own(k, _):
         rows_k = pl.ds(pl.multiple_of(k * CHUNKS, CHUNKS), CHUNKS)
         x0 = xbuf[0, k]
         for p in range(2):
@@ -183,52 +207,41 @@
                 jnp.where(lane_at == 2 * row_at + p * (FINE + 1), x0, 0.0), axis=1, keepdims=True
             )
             damp[p, rows_k, :] = jnp.broadcast_to(OMEGA / diagonal, (CHUNKS, LANES))
-        for q in range(NEAR):
-            compact[0, q, 0] = zero
-            compact[1, q, 0] = zero
-            count = counts[k, CLASS[q]]
-            word = jnp.int32(0)
-            for t in range(ROW_SLOTS):
-                slot = CLASS[q] * ROW_SLOTS + t
-                high, low = split(xbuf[slot, k])
-                compact[0, q, t + 1] = high
-                compact[1, q, t + 1] = low
-                word = word | jnp.where(t < count, (t + 1) << (columns[k, slot] * 4), 0)
-            for j in range(BLOCKS):
-                e = (word >> (4 * j)) & 7
-                lanes_j = slice(j * LANES, (j + 1) * LANES)
-                dense[q, 0, rows_k, lanes_j] = compact[0, q, e]
-                dense[q, 1, rows_k, lanes_j] = compact[1, q, e]
+        spread(0, 0, k)
         return 0
 
-    lax.fori_loop(0, BLOCKS, spread, 0)
-
-    def near_aggs(q):
-        near_row = jnp.clip(places[q][0], 0, rows - 1)
-        near_col = jnp.clip(places[q][1], 0, cols - 1)
-        first = (near_row * cols + near_col) * BLOCKS
-        return [aggs[first + j] & 1 for j in range(BLOCKS)]
-
-    def smooth(q):
-        groups = near_aggs(q)
-        for pair in range(BLOCKS // 2):
-            v = tpack[q, pair]
+    def spread_near(k, _):
+        for q in range(1, NEAR):
+            spread(q, CLASS[q] * ROW_SLOTS, k)
+        return 0
+
+    def smooth_half(q, group):
+        for pair in range(2):
+            v = tpack[q, group, pair]
             r = pltpu.roll(v, FINE, 1)
-            both = (jnp.where(low_half, v, r), jnp.where(low_half, r, v))
-            for side in range(2):
-                j = 2 * pair + side
-                high, low = split(jnp.where(half == groups[j], both[side], 0.0))
-                for p in range(2):
-                    rows_j = slice(j * LANES + p * FINE, j * LANES + (p + 1) * FINE)
-                    weights[0, rows_j, p * LANES : (p + 1) * LANES] = high
-                    weights[1, rows_j, p * LANES : (p + 1) * LANES] = low
-        s = (
-            dot(dense[q, 0], weights[0])
-            + dot(dense[q, 1], weights[0])
-            + dot(dense[q, 0], weights[1])
+            for part, (v_part, r_part) in enumerate(zip(split(v), split(r))):
+                lanes_part = slice(part * LANES, (part + 1) * LANES)
+                none = jnp.zeros_like(v_part)
+                tiles_at = (
+                    jnp.where(low_half, v_part, none),
+                    jnp.where(low_half, none, r_part),
+                    jnp.where(low_half, r_part, none),
+                    jnp.where(low_half, none, v_part),
+                )
+                for n in range(4):
+                    rows_n = slice((4 * pair + n) * FINE, (4 * pair + n + 1) * FINE)
+                    weights[group, rows_n, lanes_part] = tiles_at[n]
+        x = dot(dense[q, group], weights[group])
+        halves[q, group] = x[:256, :LANES] + (x[:256, LANES:] + x[256:, :LANES])
+
+    def finish(q):
+        s_0, s_1 = halves[q, 0], halves[q, 1]
+        by_parity = (
+            jnp.where(low_half, s_0, pltpu.roll(s_1, FINE, 1)),
+            jnp.where(low_half, pltpu.roll(s_0, FINE, 1), s_1),
         )
         for p in range(2):
-            s_p = s[:, p * LANES : (p + 1) * LANES]
+            s_p = by_parity[p]
             rows_p = slice(p * 256, (p + 1) * 256)
             high, low = split(s_p)
             right[0, rows_p, q * LANES : (q + 1) * LANES] = high
@@ -240,7 +253,7 @@
                     t_k = tp[k]
                     r_k = pltpu.roll(t_k, FINE, 1)
                     t_both = jnp.where(low_half, t_k, r_k) if p == 0 else jnp.where(low_half, r_k, t_k)
-                    own.append(jnp.where(half == groups[k], t_both, 0.0))
+                    own.append(jnp.where(half == own_groups[k], t_both, 0.0))
                 l_p = l_p + jnp.concatenate(own, axis=0)
             high, low = split(l_p.T)
             left[0, q * LANES : (q + 1) * LANES, rows_p] = high
@@ -295,43 +308,71 @@
                 for m in range(m_from, m_to):
                     piece_copy(q, m).start()
 
-    def wait_tiles(q):
+    def wait_tiles(q, group):
         @pl.when(exists[q])
         def _():
-            arrival(q).wait_recv()
-
-    smooth(0)
-    wait_tiles(1)
-    smooth(1)
-    wait_tiles(2)
-    smooth(2)
-    make_and_send(1, 3, 0, 2)
-    make_and_send(1, 3, 2, 3)
-    make_and_send(0, 1, 0, 3)
-    wait_tiles(3)
-    smooth(3)
-    wait_tiles(4)
-    smooth(4)
+            arrival(q, group).wait_recv()
+
+    pltpu.make_async_copy(xbuf.at[0:ROW_SLOTS], xbuf.at[0:ROW_SLOTS], xsem.at[0]).wait()
+    lax.fori_loop(0, BLOCKS, spread_own, 0)
+    smooth_half(0, 0)
+    smooth_half(0, 1)
+    finish(0)
+
+    pl.semaphore_wait(barrier, near_count)
+    for group in range(2):
+        for q in (3, 4, 1, 2):
+
+            @pl.when(exists[q])
+            def _():
+                tile_copy(q, group).start()
+
+    for q in range(1, NEAR):
+
+        @pl.when(jnp.logical_not(exists[q]))
+        def _():
+            tpack[q] = jnp.zeros((2, 2, FINE, LANES), F32)
+
+    for o in range(OFFSETS):
+        if o not in own_bands:
+            out[:, o * LANES : (o + 1) * LANES] = jnp.zeros((LANES, LANES), F32)
+
+    pltpu.make_async_copy(xbuf.at[ROW_SLOTS:SLOTS], xbuf.at[ROW_SLOTS:SLOTS], xsem.at[1]).wait()
+    lax.fori_loop(0, BLOCKS, spread_near, 0)
+
+    for q in (1, 2):
+        for group in range(2):
+            wait_tiles(q, group)
+            smooth_half(q, group)
+        finish(q)
+    for group in range(2):
+        for q in (3, 4):
+            wait_tiles(q, group)
+            smooth_half(q, group)
+    finish(3)
+    finish(4)
     make_and_send(3, 5, 0, 2)
     make_and_send(3, 5, 2, 4)
     make_and_send(3, 5, 4, 5)
-    make_and_send(1, 3, 3, 5)
-    make_and_send(0, 1, 3, 5)
-    for q_group, m_group in (((1, 2), range(0, 3)), ((3, 4), range(0, 3)), ((1, 2), range(3, 5)), ((3, 4), range(3, 5))):
-        for m in m_group:
-            for q in q_group:
-
-                @pl.when(exists[q])
-                def _():
-                    piece_arrival(q, m).wait_recv()
-                    o = band_of(q, m)
-                    out[:, o * LANES : (o + 1) * LANES] += grecv[q, m]
+    make_and_send(1, 3, 0, 2)
+    make_and_send(1, 3, 2, 4)
+    make_and_send(1, 3, 4, 5)
+    make_and_send(0, 1, 0, 5)
+    for m in range(NEAR):
+        for q in (1, 2, 3, 4):
+
+            @pl.when(exists[q])
+            def _():
+                piece_arrival(q, m).wait_recv()
+                o = band_of(q, m)
+                out[:, o * LANES : (o + 1) * LANES] += grecv[q, m]
 
     for q in range(1, NEAR):
 
         @pl.when(exists[q])
         def _():
-            tile_copy(q).wait_send()
+            for group in range(2):
+                tile_copy(q, group).wait_send()
             for m in range(NEAR):
                 piece_copy(q, m).wait_send()
 
@@ -353,21 +394,23 @@
                 pltpu.SMEM((BLOCKS, NEAR), jnp.int32),
                 pltpu.SMEM(aggregate_of.shape, jnp.int32),
                 pltpu.VMEM((SLOTS, BLOCKS, CHUNKS, LANES), F32),
-                pltpu.VMEM((2, NEAR, ROW_SLOTS + 1, CHUNKS, LANES), BF16),
-                pltpu.VMEM((NEAR, 2, BLOCKS * CHUNKS, BLOCKS * LANES), BF16),
+                pltpu.VMEM((NEAR, 2, 8, CHUNKS, LANES), BF16),
+                pltpu.VMEM((NEAR, 2, 2 * BLOCKS * CHUNKS, 4 * LANES), BF16),
+                pltpu.SMEM((NEAR, BLOCKS), jnp.int32),
                 pltpu.VMEM((BLOCKS, CHUNKS, LANES), F32),
-                pltpu.VMEM((NEAR, BLOCKS // 2, FINE, LANES), F32),
-                pltpu.VMEM((2, BLOCKS * LANES, 2 * LANES), BF16),
+                pltpu.VMEM((NEAR, 2, 2, FINE, LANES), F32),
+                pltpu.VMEM((2, 4 * LANES, 2 * LANES), BF16),
+                pltpu.VMEM((NEAR, 2, BLOCKS * CHUNKS, LANES), F32),
                 pltpu.VMEM((2, BLOCKS * CHUNKS, LANES), F32),
                 pltpu.VMEM((2, BLOCKS * FINE, NEAR * LANES), BF16),
                 pltpu.VMEM((2, NEAR * LANES, BLOCKS * FINE), BF16),
                 pltpu.VMEM((NEAR, NEAR, LANES, LANES), F32),
                 pltpu.VMEM((NEAR, NEAR, LANES, LANES), F32),
-                dma,
+                dma((2,)),
                 dma,
                 dma((3,)),
-                dma((NEAR,)),
-                dma((NEAR,)),
+                dma((NEAR, 2)),
+                dma((NEAR, 2)),
                 dma((NEAR, NEAR)),
                 dma((NEAR, NEAR)),
             ],

time: 24.2 us -> 22.7 us (0.938)
  Pallas kernels: 22.9 us -> 21.4 us
    pallas_call x1, Pallas kernels: 22.9 us -> 21.4 us  [body(): pl.pallas_call(lambda *refs: kernel(rows, cols, *refs), out_shape=jax.Sha...]
where the time goes in v3:
time: 22.7 us; the launch traced here: 22.4 us
  Pallas kernels  21.4 us (94%)
  local copies, waits for them, and re-layouts  0.9 us (4%)
    pallas_call x1, Pallas kernels, body(): pl.pallas_call(lambda *refs: kernel(rows, cols, *refs), out_shape=jax.Sha...  21.4 us
    unnamed x1, local copies, waits for them, and re-layouts  0.9 us

profile of v3, /device:TPU:25, one launch (start us, length us, event | category | flops | bytes accessed | tf_op | source)
XLA Modules:
  0.0 22.4 jit_solution(16690841206459142629)
XLA Ops:
  0.0 21.4 %shard_map.55 = f32[128,1664]{1,0:T(8,128)S(1)} custom-call(f32[20,8,4096]{2,1,0:T(8,128)} %bitcast.3, s32[8,20]{1,0:T(8,128)} %refs_1_.1, s32[8,5]{1,0:T(8,128)} %refs_2_.1, f32[8,4096]{1,0:T(8,128)} %refs_3_.1, s32[1024]{0:T(1024)} %refs_4_.1), custom_call_target="tpu_custom_call" | custom-call | tf_op jit(solution)/shard_map/pallas_call | solution.py:387
  21.4 0.9 %copy.7 = f32[2,64,1664]{2,1,0:T(8,128)} copy(f32[2,64,1664]{2,1,0:T(8,128)S(1)} %bitcast.2) | data formatting | bytes 1703936

commit v4 on v3

--- a/solution.py
+++ b/solution.py
@@ -17,31 +17,11 @@
 LANES = 128
 OMEGA = 2.0 / 3.0
 
-STEPS = ((0, 0), (-1, 0), (1, 0), (0, -1), (0, 1))
-CLASS = (0, 3, 4, 1, 2)
-OPPOSITE = (0, 2, 1, 4, 3)
-BAND_STEPS = (
-    (-2, 0),
-    (-1, -1),
-    (-1, 0),
-    (-1, 1),
-    (0, -2),
-    (0, -1),
-    (0, 0),
-    (0, 1),
-    (0, 2),
-    (1, -1),
-    (1, 0),
-    (1, 1),
-    (2, 0),
-)
+ROW_STEPS = (0, 1, -1, 0, 0)
+COL_STEPS = (0, 0, 0, -1, 1)
+OPPOSITE = (0, 1, 2, 4, 3)
 OFFSETS = 13
 NEAR = 5
-
-
-def band_of(source, target):
-    a, b = STEPS[source], STEPS[target]
-    return BAND_STEPS.index((a[0] + b[0], a[1] + b[1]))
 
 
 def dot(a, b):
@@ -88,21 +68,55 @@
 ):
     my_row = lax.axis_index("row")
     my_col = lax.axis_index("col")
-    places = [(my_row + s[0], my_col + s[1]) for s in STEPS]
+    even = lax.rem(my_row, 2) == 0
+    sign = jnp.where(even, 1, -1)
+    places = [(my_row + sign * ROW_STEPS[q], my_col + COL_STEPS[q]) for q in range(NEAR)]
     exists = [
-        None,
-        my_row > 0,
-        my_row < rows - 1,
+        True,
+        True,
+        (places[2][0] >= 0) & (places[2][0] < rows),
         my_col > 0,
         my_col < cols - 1,
     ]
+    first_slots = [
+        0,
+        jnp.where(even, 16, 12),
+        jnp.where(even, 12, 16),
+        4,
+        8,
+    ]
+
+    def band(row_units, col_step):
+        if row_units == 0:
+            return 6 + col_step
+        ahead, behind = {1: (10, 2), -1: (2, 10), 2: (12, 0), -2: (0, 12)}[row_units]
+        return jnp.where(even, ahead, behind) + col_step
+
+    def band_of(q, m):
+        turn = -1 if q in (1, 2) else 1
+        return band(ROW_STEPS[q] + turn * ROW_STEPS[m], COL_STEPS[q] + COL_STEPS[m])
+
+    def lanes_of(o):
+        if isinstance(o, int):
+            return slice(o * LANES, (o + 1) * LANES)
+        return pl.ds(pl.multiple_of(o * LANES, LANES), LANES)
+
+    def when_there(q):
+        def run(f):
+            if exists[q] is True:
+                f()
+            else:
+                pl.when(exists[q])(f)
+
+        return run
 
     barrier = pltpu.get_barrier_semaphore()
-    near_count = jnp.int32(0)
+    near_count = jnp.int32(1)
     for q in range(1, NEAR):
-        near_count = near_count + jnp.where(exists[q], 1, 0)
-
-        @pl.when(exists[q])
+        if q > 1:
+            near_count = near_count + jnp.where(exists[q], 1, 0)
+
+        @when_there(q)
         def _():
             pl.semaphore_signal(barrier, inc=1, device_id=places[q], device_id_type=MESH)
 
@@ -123,7 +137,6 @@
 
     lane = lax.broadcasted_iota(jnp.int32, (1, LANES), 1)
     low_half = lane < FINE
-    half = jnp.where(low_half, 0, 1)
 
     for copy in small:
         copy.wait()
@@ -172,8 +185,6 @@
             device_id_type=MESH,
         )
 
-    own_bands = [band_of(0, m) for m in range(NEAR)]
-
     row_at = lax.broadcasted_iota(jnp.int32, (CHUNKS, LANES), 0)
     lane_at = lax.broadcasted_iota(jnp.int32, (CHUNKS, LANES), 1)
 
@@ -182,7 +193,8 @@
         compact[q, 0, 0] = zero
         compact[q, 1, 0] = zero
 
-    def spread(q, slots, k):
+    def spread(q, k):
+        slots = first_slots[q]
         rows_k = pl.ds(pl.multiple_of(k * CHUNKS, CHUNKS), CHUNKS)
         rows_low = pl.ds(pl.multiple_of(k * CHUNKS + 256, CHUNKS), CHUNKS)
         count = counts[k, slots // ROW_SLOTS]
@@ -200,19 +212,21 @@
                 dense[q, group, rows_low, lanes_n] = compact[q, 1, e]
 
     def spread_own(k, _):
-        rows_k = pl.ds(pl.multiple_of(k * CHUNKS, CHUNKS), CHUNKS)
         x0 = xbuf[0, k]
-        for p in range(2):
-            diagonal = jnp.sum(
+        diagonal = [
+            jnp.sum(
                 jnp.where(lane_at == 2 * row_at + p * (FINE + 1), x0, 0.0), axis=1, keepdims=True
             )
-            damp[p, rows_k, :] = jnp.broadcast_to(OMEGA / diagonal, (CHUNKS, LANES))
-        spread(0, 0, k)
+            for p in range(2)
+        ]
+        rows_k = pl.ds(pl.multiple_of(k * CHUNKS, CHUNKS), CHUNKS)
+        damp[rows_k, :] = OMEGA / jnp.where(low_half, diagonal[0], diagonal[1])
+        spread(0, k)
         return 0
 
     def spread_near(k, _):
         for q in range(1, NEAR):
-            spread(q, CLASS[q] * ROW_SLOTS, k)
+            spread(q, k)
         return 0
 
     def smooth_half(q, group):
@@ -230,151 +244,165 @@
                 )
                 for n in range(4):
                     rows_n = slice((4 * pair + n) * FINE, (4 * pair + n + 1) * FINE)
-                    weights[group, rows_n, lanes_part] = tiles_at[n]
-        x = dot(dense[q, group], weights[group])
-        halves[q, group] = x[:256, :LANES] + (x[:256, LANES:] + x[256:, :LANES])
-
-    def finish(q):
+                    weights[q, group, rows_n, lanes_part] = tiles_at[n]
+        x = dot(dense[q, group, :256], weights[q, group])
+        y = dot(dense[q, group, 256:], weights[q, group, :, :LANES])
+        s = x[:, :LANES] + (x[:, LANES:] + y)
+        halves[q, group] = s
+        l = -(damp[...] * s)
+        if q == 0:
+            own = [jnp.where(own_groups[k] == group, tp[k], 0.0) for k in range(BLOCKS)]
+            l = l + jnp.concatenate(own, axis=0)
+        first = q * LANES + group * FINE
+        for part, l_part in enumerate(split(l.T)):
+            for p in range(2):
+                left[part, first : first + FINE, p * 256 : (p + 1) * 256] = l_part[p * FINE : (p + 1) * FINE]
+
+    def make_right(q):
         s_0, s_1 = halves[q, 0], halves[q, 1]
         by_parity = (
             jnp.where(low_half, s_0, pltpu.roll(s_1, FINE, 1)),
             jnp.where(low_half, pltpu.roll(s_0, FINE, 1), s_1),
         )
         for p in range(2):
-            s_p = by_parity[p]
-            rows_p = slice(p * 256, (p + 1) * 256)
-            high, low = split(s_p)
-            right[0, rows_p, q * LANES : (q + 1) * LANES] = high
-            right[1, rows_p, q * LANES : (q + 1) * LANES] = low
-            l_p = -(damp[p] * s_p)
-            if q == 0:
-                own = []
-                for k in range(BLOCKS):
-                    t_k = tp[k]
-                    r_k = pltpu.roll(t_k, FINE, 1)
-                    t_both = jnp.where(low_half, t_k, r_k) if p == 0 else jnp.where(low_half, r_k, t_k)
-                    own.append(jnp.where(half == own_groups[k], t_both, 0.0))
-                l_p = l_p + jnp.concatenate(own, axis=0)
-            high, low = split(l_p.T)
-            left[0, q * LANES : (q + 1) * LANES, rows_p] = high
-            left[1, q * LANES : (q + 1) * LANES, rows_p] = low
-
-    def products(q_from, q_to, m_from, m_to):
-        rows_l = slice(q_from * LANES, q_to * LANES)
+            for part, r_part in enumerate(split(by_parity[p])):
+                right[part, p * 256 : (p + 1) * 256, lanes_of(q)] = r_part
+
+    def smooth(q):
+        smooth_half(q, 0)
+        smooth_half(q, 1)
+        make_right(q)
+
+    def products(row_list, m_from, m_to):
         cols_r = slice(m_from * LANES, m_to * LANES)
+        highs = jnp.concatenate([left[0, a : a + n, :] for a, n in row_list], axis=0)
+        lows = jnp.concatenate([left[1, a : a + n, :] for a, n in row_list], axis=0)
         return (
-            dot(left[0, rows_l, :], right[0, :, cols_r])
-            + dot(left[1, rows_l, :], right[0, :, cols_r])
-            + dot(left[0, rows_l, :], right[1, :, cols_r])
-        )
-
-    def piece_copy(q, m):
+            dot(highs, right[0, :, cols_r])
+            + dot(lows, right[0, :, cols_r])
+            + dot(highs, right[1, :, cols_r])
+        )
+
+    def piece(q, m, group, to):
+        at = pl.ds(0, LANES) if group is None else pl.ds(group * FINE, FINE)
+        spot = group or 0
         return pltpu.make_async_remote_copy(
-            src_ref=gsend.at[q, m],
-            dst_ref=grecv.at[OPPOSITE[q], m],
-            send_sem=gsend_sem.at[q, m],
-            recv_sem=grecv_sem.at[OPPOSITE[q], m],
+            src_ref=gsend.at[q, m, at],
+            dst_ref=grecv.at[to, m, at],
+            send_sem=gsend_sem.at[q, m, spot],
+            recv_sem=grecv_sem.at[to, m, spot],
             device_id=places[q],
             device_id_type=MESH,
         )
 
-    def piece_arrival(q, m):
-        return pltpu.make_async_remote_copy(
-            src_ref=gsend.at[q, m],
-            dst_ref=grecv.at[q, m],
-            send_sem=gsend_sem.at[q, m],
-            recv_sem=grecv_sem.at[q, m],
-            device_id=places[q],
-            device_id_type=MESH,
-        )
-
-    def make_and_send(q_from, q_to, m_from, m_to):
-        g = products(q_from, q_to, m_from, m_to)
-        for q in range(q_from, q_to):
+    def piece_copy(q, m, group):
+        return piece(q, m, group, OPPOSITE[q])
+
+    def piece_arrival(q, m, group):
+        return piece(q, m, group, q)
+
+    def start_pieces(q, m_from, m_to, group):
+        @when_there(q)
+        def _():
             for m in range(m_from, m_to):
-                part = g[
-                    (q - q_from) * LANES : (q - q_from + 1) * LANES,
-                    (m - m_from) * LANES : (m - m_from + 1) * LANES,
-                ]
+                piece_copy(q, m, group).start()
+
+    def make_and_send(q_list, m_from, m_to):
+        g = products([(q * LANES, LANES) for q in q_list], m_from, m_to)
+        for at, q in enumerate(q_list):
+            for m in range(m_from, m_to):
+                part = g[at * LANES : (at + 1) * LANES, (m - m_from) * LANES : (m - m_from + 1) * LANES]
                 if q == 0:
-                    o = own_bands[m]
-                    out[:, o * LANES : (o + 1) * LANES] = part
+                    out[:, lanes_of(band_of(0, m))] = part
                 else:
                     gsend[q, m] = part
-        for q in range(max(q_from, 1), q_to):
-
-            @pl.when(exists[q])
-            def _():
-                for m in range(m_from, m_to):
-                    piece_copy(q, m).start()
+        for q in q_list:
+            if q > 0:
+                start_pieces(q, m_from, m_to, None)
+
+    def make_and_send_halves(group, m_from, m_to):
+        g = products([(q * LANES + group * FINE, FINE) for q in (3, 4)], m_from, m_to)
+        for at, q in enumerate((3, 4)):
+            for m in range(m_from, m_to):
+                gsend[q, m, group * FINE : (group + 1) * FINE] = g[
+                    at * FINE : (at + 1) * FINE, (m - m_from) * LANES : (m - m_from + 1) * LANES
+                ]
+        for q in (3, 4):
+            start_pieces(q, m_from, m_to, group)
 
     def wait_tiles(q, group):
-        @pl.when(exists[q])
+        @when_there(q)
         def _():
             arrival(q, group).wait_recv()
 
-    pltpu.make_async_copy(xbuf.at[0:ROW_SLOTS], xbuf.at[0:ROW_SLOTS], xsem.at[0]).wait()
-    lax.fori_loop(0, BLOCKS, spread_own, 0)
-    smooth_half(0, 0)
-    smooth_half(0, 1)
-    finish(0)
-
     pl.semaphore_wait(barrier, near_count)
     for group in range(2):
-        for q in (3, 4, 1, 2):
-
-            @pl.when(exists[q])
+        for q in (3, 4, 2, 1):
+
+            @when_there(q)
             def _():
                 tile_copy(q, group).start()
 
-    for q in range(1, NEAR):
+    for q in range(2, NEAR):
 
         @pl.when(jnp.logical_not(exists[q]))
         def _():
             tpack[q] = jnp.zeros((2, 2, FINE, LANES), F32)
 
     for o in range(OFFSETS):
-        if o not in own_bands:
-            out[:, o * LANES : (o + 1) * LANES] = jnp.zeros((LANES, LANES), F32)
-
+        if o not in (2, 5, 6, 7, 10):
+            out[:, lanes_of(o)] = jnp.zeros((LANES, LANES), F32)
+
+    pltpu.make_async_copy(xbuf.at[0:ROW_SLOTS], xbuf.at[0:ROW_SLOTS], xsem.at[0]).wait()
+    lax.fori_loop(0, BLOCKS, spread_own, 0)
     pltpu.make_async_copy(xbuf.at[ROW_SLOTS:SLOTS], xbuf.at[ROW_SLOTS:SLOTS], xsem.at[1]).wait()
     lax.fori_loop(0, BLOCKS, spread_near, 0)
-
-    for q in (1, 2):
-        for group in range(2):
-            wait_tiles(q, group)
-            smooth_half(q, group)
-        finish(q)
+    smooth(0)
+    wait_tiles(1, 0)
+    wait_tiles(1, 1)
+    smooth(1)
+    make_and_send((1,), 0, 2)
+    make_and_send((0,), 0, 2)
     for group in range(2):
-        for q in (3, 4):
-            wait_tiles(q, group)
-            smooth_half(q, group)
-    finish(3)
-    finish(4)
-    make_and_send(3, 5, 0, 2)
-    make_and_send(3, 5, 2, 4)
-    make_and_send(3, 5, 4, 5)
-    make_and_send(1, 3, 0, 2)
-    make_and_send(1, 3, 2, 4)
-    make_and_send(1, 3, 4, 5)
-    make_and_send(0, 1, 0, 5)
-    for m in range(NEAR):
-        for q in (1, 2, 3, 4):
-
-            @pl.when(exists[q])
-            def _():
-                piece_arrival(q, m).wait_recv()
-                o = band_of(q, m)
-                out[:, o * LANES : (o + 1) * LANES] += grecv[q, m]
+        wait_tiles(3, group)
+        wait_tiles(4, group)
+        smooth_half(3, group)
+        smooth_half(4, group)
+        make_and_send_halves(group, 0, 2)
+    wait_tiles(2, 0)
+    wait_tiles(2, 1)
+    smooth(2)
+    make_and_send((2,), 0, 2)
+    make_right(3)
+    make_right(4)
+    make_and_send((3, 4), 2, 4)
+    make_and_send((3, 4), 4, 5)
+    make_and_send((2,), 2, 5)
+    make_and_send((1,), 2, 5)
+    make_and_send((0,), 2, 5)
+
+    def groups_of(q, m):
+        return (0, 1) if q in (3, 4) and m < 2 else (None,)
+
+    for q_list, m_list in (((1,), (0, 1)), ((3, 4), (0, 1)), ((1,), (2, 3, 4)), ((2, 3, 4), (2, 3)), ((2,), (0, 1)), ((2, 3, 4), (4,))):
+        for m in m_list:
+            for q in q_list:
+
+                @when_there(q)
+                def _():
+                    for group in groups_of(q, m):
+                        piece_arrival(q, m, group).wait_recv()
+                    out[:, lanes_of(band_of(q, m))] += grecv[q, m]
 
     for q in range(1, NEAR):
 
-        @pl.when(exists[q])
+        @when_there(q)
         def _():
             for group in range(2):
                 tile_copy(q, group).wait_send()
             for m in range(NEAR):
-                piece_copy(q, m).wait_send()
+                for group in groups_of(q, m):
+                    piece_copy(q, m, group).wait_send()
 
 
 def solution(mesh):
@@ -399,9 +427,9 @@
                 pltpu.SMEM((NEAR, BLOCKS), jnp.int32),
                 pltpu.VMEM((BLOCKS, CHUNKS, LANES), F32),
                 pltpu.VMEM((NEAR, 2, 2, FINE, LANES), F32),
-                pltpu.VMEM((2, 4 * LANES, 2 * LANES), BF16),
+                pltpu.VMEM((NEAR, 2, 4 * LANES, 2 * LANES), BF16),
                 pltpu.VMEM((NEAR, 2, BLOCKS * CHUNKS, LANES), F32),
-                pltpu.VMEM((2, BLOCKS * CHUNKS, LANES), F32),
+                pltpu.VMEM((BLOCKS * CHUNKS, LANES), F32),
                 pltpu.VMEM((2, BLOCKS * FINE, NEAR * LANES), BF16),
                 pltpu.VMEM((2, NEAR * LANES, BLOCKS * FINE), BF16),
                 pltpu.VMEM((NEAR, NEAR, LANES, LANES), F32),
@@ -411,8 +439,8 @@
                 dma((3,)),
                 dma((NEAR, 2)),
                 dma((NEAR, 2)),
-                dma((NEAR, NEAR)),
-                dma((NEAR, NEAR)),
+                dma((NEAR, NEAR, 2)),
+                dma((NEAR, NEAR, 2)),
             ],
             compiler_params=pltpu.CompilerParams(
                 collective_id=0, has_side_effects=True, vmem_limit_bytes=40 << 20

time: 22.7 us -> 20.5 us (0.903)
  Pallas kernels: 21.4 us -> 19.2 us
    pallas_call x1, Pallas kernels: 21.4 us -> 19.2 us  [body(): pl.pallas_call(lambda *refs: kernel(rows, cols, *refs), out_shape=jax.Sha...]
where the time goes in v4:
time: 20.5 us; the launch traced here: 20.1 us
  Pallas kernels  19.2 us (94%)
  local copies, waits for them, and re-layouts  0.9 us (4%)
    pallas_call x1, Pallas kernels, body(): pl.pallas_call(lambda *refs: kernel(rows, cols, *refs), out_shape=jax.Sha...  19.2 us
    unnamed x1, local copies, waits for them, and re-layouts  0.9 us

profile of v4, /device:TPU:25, one launch (start us, length us, event | category | flops | bytes accessed | tf_op | source)
XLA Modules:
  0.0 20.1 jit_solution(15965364848302526784)
XLA Ops:
  0.0 19.2 %shard_map.55 = f32[128,1664]{1,0:T(8,128)S(1)} custom-call(f32[20,8,4096]{2,1,0:T(8,128)} %bitcast.3, s32[8,20]{1,0:T(8,128)} %refs_1_.1, s32[8,5]{1,0:T(8,128)} %refs_2_.1, f32[8,4096]{1,0:T(8,128)} %refs_3_.1, s32[1024]{0:T(1024)} %refs_4_.1), custom_call_target="tpu_custom_call" | custom-call | tf_op jit(solution)/shard_map/pallas_call | solution.py:415
  19.2 0.9 %copy.7 = f32[2,64,1664]{2,1,0:T(8,128)} copy(f32[2,64,1664]{2,1,0:T(8,128)S(1)} %bitcast.2) | data formatting | bytes 1703936

commit v5 on v4

--- a/solution.py
+++ b/solution.py
@@ -22,6 +22,7 @@
 OPPOSITE = (0, 1, 2, 4, 3)
 OFFSETS = 13
 NEAR = 5
+X_CHIPS = 4
 
 
 def dot(a, b):
@@ -110,6 +111,8 @@
 
         return run
 
+    left_far = lax.rem(my_col, X_CHIPS) == 0
+
     barrier = pltpu.get_barrier_semaphore()
     near_count = jnp.int32(1)
     for q in range(1, NEAR):
@@ -169,8 +172,8 @@
         return pltpu.make_async_remote_copy(
             src_ref=tpack.at[0, group],
             dst_ref=tpack.at[OPPOSITE[q], group],
-            send_sem=tsend.at[q, group],
-            recv_sem=trecv.at[OPPOSITE[q], group],
+            send_sem=tsend.at[q - 1],
+            recv_sem=trecv.at[OPPOSITE[q] - 1, group],
             device_id=places[q],
             device_id_type=MESH,
         )
@@ -179,8 +182,8 @@
         return pltpu.make_async_remote_copy(
             src_ref=tpack.at[0, group],
             dst_ref=tpack.at[q, group],
-            send_sem=tsend.at[q, group],
-            recv_sem=trecv.at[q, group],
+            send_sem=tsend.at[q - 1],
+            recv_sem=trecv.at[q - 1, group],
             device_id=places[q],
             device_id_type=MESH,
         )
@@ -283,23 +286,37 @@
             + dot(highs, right[1, :, cols_r])
         )
 
-    def piece(q, m, group, to):
+    def piece_copy(q, m, group):
         at = pl.ds(0, LANES) if group is None else pl.ds(group * FINE, FINE)
-        spot = group or 0
         return pltpu.make_async_remote_copy(
             src_ref=gsend.at[q, m, at],
-            dst_ref=grecv.at[to, m, at],
-            send_sem=gsend_sem.at[q, m, spot],
-            recv_sem=grecv_sem.at[to, m, spot],
+            dst_ref=grecv.at[OPPOSITE[q], m, at],
+            send_sem=gsend_sem.at[q - 1],
+            recv_sem=grecv_sem.at[OPPOSITE[q] - 1, m // 2],
             device_id=places[q],
             device_id_type=MESH,
         )
 
-    def piece_copy(q, m, group):
-        return piece(q, m, group, OPPOSITE[q])
-
-    def piece_arrival(q, m, group):
-        return piece(q, m, group, q)
+    def set_arrival(q, m_from, m_to):
+        return pltpu.make_async_remote_copy(
+            src_ref=gsend.at[q, m_from:m_to],
+            dst_ref=grecv.at[q, m_from:m_to],
+            send_sem=gsend_sem.at[q - 1],
+            recv_sem=grecv_sem.at[q - 1, m_from // 2],
+            device_id=places[q],
+            device_id_type=MESH,
+        )
+
+    def all_sent(q):
+        pltpu.make_async_remote_copy(
+            src_ref=tpack.at[0],
+            dst_ref=tpack.at[OPPOSITE[q]],
+            send_sem=tsend.at[q - 1],
+            recv_sem=trecv.at[q - 1, 0],
+            device_id=places[q],
+            device_id_type=MESH,
+        ).wait_send()
+        set_arrival(q, 0, NEAR).wait_send()
 
     def start_pieces(q, m_from, m_to, group):
         @when_there(q)
@@ -316,9 +333,12 @@
                     out[:, lanes_of(band_of(0, m))] = part
                 else:
                     gsend[q, m] = part
-        for q in q_list:
-            if q > 0:
-                start_pieces(q, m_from, m_to, None)
+        if q_list == (3, 4):
+            far_first(lambda q: start_pieces(q, m_from, m_to, None))
+        else:
+            for q in q_list:
+                if q > 0:
+                    start_pieces(q, m_from, m_to, None)
 
     def make_and_send_halves(group, m_from, m_to):
         g = products([(q * LANES + group * FINE, FINE) for q in (3, 4)], m_from, m_to)
@@ -327,8 +347,7 @@
                 gsend[q, m, group * FINE : (group + 1) * FINE] = g[
                     at * FINE : (at + 1) * FINE, (m - m_from) * LANES : (m - m_from + 1) * LANES
                 ]
-        for q in (3, 4):
-            start_pieces(q, m_from, m_to, group)
+        far_first(lambda q: start_pieces(q, m_from, m_to, group))
 
     def wait_tiles(q, group):
         @when_there(q)
@@ -336,12 +355,26 @@
             arrival(q, group).wait_recv()
 
     pl.semaphore_wait(barrier, near_count)
+    def send_tiles(q, group):
+        @when_there(q)
+        def _():
+            tile_copy(q, group).start()
+
+    def far_first(send):
+        @pl.when(left_far)
+        def _():
+            send(3)
+            send(4)
+
+        @pl.when(jnp.logical_not(left_far))
+        def _():
+            send(4)
+            send(3)
+
     for group in range(2):
-        for q in (3, 4, 2, 1):
-
-            @when_there(q)
-            def _():
-                tile_copy(q, group).start()
+        far_first(lambda q: send_tiles(q, group))
+        for q in (2, 1):
+            send_tiles(q, group)
 
     for q in range(2, NEAR):
 
@@ -381,28 +414,30 @@
     make_and_send((1,), 2, 5)
     make_and_send((0,), 2, 5)
 
-    def groups_of(q, m):
-        return (0, 1) if q in (3, 4) and m < 2 else (None,)
-
-    for q_list, m_list in (((1,), (0, 1)), ((3, 4), (0, 1)), ((1,), (2, 3, 4)), ((2, 3, 4), (2, 3)), ((2,), (0, 1)), ((2, 3, 4), (4,))):
-        for m in m_list:
-            for q in q_list:
-
-                @when_there(q)
-                def _():
-                    for group in groups_of(q, m):
-                        piece_arrival(q, m, group).wait_recv()
+    for q_list, m_from, m_to in (
+        ((1,), 0, 2),
+        ((3, 4), 0, 2),
+        ((1,), 2, 4),
+        ((1,), 4, 5),
+        ((2,), 0, 2),
+        ((3, 4), 2, 4),
+        ((2,), 2, 4),
+        ((2,), 4, 5),
+        ((3, 4), 4, 5),
+    ):
+        for q in q_list:
+
+            @when_there(q)
+            def _():
+                set_arrival(q, m_from, m_to).wait_recv()
+                for m in range(m_from, m_to):
                     out[:, lanes_of(band_of(q, m))] += grecv[q, m]
 
     for q in range(1, NEAR):
 
         @when_there(q)
         def _():
-            for group in range(2):
-                tile_copy(q, group).wait_send()
-            for m in range(NEAR):
-                for group in groups_of(q, m):
-                    piece_copy(q, m, group).wait_send()
+            all_sent(q)
 
 
 def solution(mesh):
@@ -437,10 +472,10 @@
                 dma((2,)),
                 dma,
                 dma((3,)),
-                dma((NEAR, 2)),
-                dma((NEAR, 2)),
-                dma((NEAR, NEAR, 2)),
-                dma((NEAR, NEAR, 2)),
+                dma((NEAR - 1,)),
+                dma((NEAR - 1, 2)),
+                dma((NEAR - 1,)),
+                dma((NEAR - 1, 3)),
             ],
             compiler_params=pltpu.CompilerParams(
                 collective_id=0, has_side_effects=True, vmem_limit_bytes=40 << 20

time: 20.5 us -> 19.7 us (0.961)
  the two profiles are of different devices: /device:TPU:25 before, /device:TPU:24 now
where the time goes in v5:
time: 19.7 us; the launch traced here: 19.5 us
  Pallas kernels  18.6 us (94%)
  local copies, waits for them, and re-layouts  0.9 us (5%)
    pallas_call x1, Pallas kernels, body(): pl.pallas_call(lambda *refs: kernel(rows, cols, *refs), out_shape=jax.Sha...  18.6 us
    unnamed x1, local copies, waits for them, and re-layouts  0.9 us

profile of v5, /device:TPU:24, one launch (start us, length us, event | category | flops | bytes accessed | tf_op | source)
XLA Modules:
  0.0 19.5 jit_solution(11169919803098522012)
XLA Ops:
  0.0 18.6 %shard_map.55 = f32[128,1664]{1,0:T(8,128)S(1)} custom-call(f32[20,8,4096]{2,1,0:T(8,128)} %bitcast.3, s32[8,20]{1,0:T(8,128)} %refs_1_.1, s32[8,5]{1,0:T(8,128)} %refs_2_.1, f32[8,4096]{1,0:T(8,128)} %refs_3_.1, s32[1024]{0:T(1024)} %refs_4_.1), custom_call_target="tpu_custom_call" | custom-call | tf_op jit(solution)/shard_map/pallas_call | solution.py:450
  18.6 0.9 %copy.7 = f32[2,64,1664]{2,1,0:T(8,128)} copy(f32[2,64,1664]{2,1,0:T(8,128)S(1)} %bitcast.2) | data formatting | bytes 1703936

commit v6 on v5

--- a/solution.py
+++ b/solution.py
@@ -59,12 +59,15 @@
     left,
     gsend,
     grecv,
+    psend,
+    precv,
     xsem,
     tsem,
     ssem,
     tsend,
     trecv,
     gsend_sem,
+    psend_sem,
     grecv_sem,
 ):
     my_row = lax.axis_index("row")
@@ -286,23 +289,58 @@
             + dot(highs, right[1, :, cols_r])
         )
 
+    square_row = lax.broadcasted_iota(jnp.int32, (FINE, FINE), 0)
+    square_col = lax.broadcasted_iota(jnp.int32, (FINE, FINE), 1)
+
+    def packed(g):
+        a, b, c = g[:FINE, :FINE], g[:FINE, FINE:], g[FINE:, FINE:]
+        square = jnp.where(square_row >= square_col, a, c)
+        diagonal = jnp.sum(jnp.where(square_row == square_col, c, 0.0), axis=0, keepdims=True)
+        top = jnp.concatenate([square, b], axis=1)
+        last = jnp.broadcast_to(jnp.concatenate([diagonal, diagonal], axis=1), (8, LANES))
+        return jnp.concatenate([top, last], axis=0)
+
+    def unpacked(x):
+        square, b = x[:FINE, :FINE], x[:FINE, FINE:]
+        diagonal = x[FINE : FINE + 1, :FINE]
+        turned = x[:FINE].T
+        square_t, b_t = turned[:FINE], turned[FINE:]
+        a = jnp.where(square_row >= square_col, square, square_t)
+        c = jnp.where(square_row < square_col, square, square_t)
+        c = jnp.where(square_row == square_col, diagonal, c)
+        return jnp.concatenate(
+            [jnp.concatenate([a, b], axis=1), jnp.concatenate([b_t, c], axis=1)], axis=0
+        )
+
     def piece_copy(q, m, group):
+        to = OPPOSITE[q]
+        recv_sem = grecv_sem.at[to - 1, max(m - 1, 0)]
+        if m == q and q > 2:
+            return pltpu.make_async_remote_copy(
+                src_ref=psend.at[q - 1],
+                dst_ref=precv.at[to - 1],
+                send_sem=psend_sem.at[q - 1],
+                recv_sem=recv_sem,
+                device_id=places[q],
+                device_id_type=MESH,
+            )
         at = pl.ds(0, LANES) if group is None else pl.ds(group * FINE, FINE)
         return pltpu.make_async_remote_copy(
             src_ref=gsend.at[q, m, at],
-            dst_ref=grecv.at[OPPOSITE[q], m, at],
+            dst_ref=grecv.at[to, m, at],
             send_sem=gsend_sem.at[q - 1],
-            recv_sem=grecv_sem.at[OPPOSITE[q] - 1, m // 2],
+            recv_sem=recv_sem,
             device_id=places[q],
             device_id_type=MESH,
         )
 
     def set_arrival(q, m_from, m_to):
+        alone = m_from == OPPOSITE[q] and q > 2
         return pltpu.make_async_remote_copy(
-            src_ref=gsend.at[q, m_from:m_to],
-            dst_ref=grecv.at[q, m_from:m_to],
+            src_ref=psend.at[q - 1] if alone else gsend.at[q, m_from:m_to],
+            dst_ref=precv.at[q - 1] if alone else grecv.at[q, m_from:m_to],
             send_sem=gsend_sem.at[q - 1],
-            recv_sem=grecv_sem.at[q - 1, m_from // 2],
+            recv_sem=grecv_sem.at[q - 1, max(m_from - 1, 0)],
             device_id=places[q],
             device_id_type=MESH,
         )
@@ -316,12 +354,21 @@
             device_id=places[q],
             device_id_type=MESH,
         ).wait_send()
-        set_arrival(q, 0, NEAR).wait_send()
+        pltpu.make_async_remote_copy(
+            src_ref=gsend.at[q, 0:4] if q > 2 else gsend.at[q],
+            dst_ref=grecv.at[q, 0:4] if q > 2 else grecv.at[q],
+            send_sem=gsend_sem.at[q - 1],
+            recv_sem=grecv_sem.at[q - 1, 0],
+            device_id=places[q],
+            device_id_type=MESH,
+        ).wait_send()
+        if q > 2:
+            piece_copy(q, q, None).wait_send()
 
     def start_pieces(q, m_from, m_to, group):
         @when_there(q)
         def _():
-            for m in range(m_from, m_to):
+            for m in sorted(range(m_from, m_to), key=lambda m: m != q):
                 piece_copy(q, m, group).start()
 
     def make_and_send(q_list, m_from, m_to):
@@ -331,6 +378,8 @@
                 part = g[at * LANES : (at + 1) * LANES, (m - m_from) * LANES : (m - m_from + 1) * LANES]
                 if q == 0:
                     out[:, lanes_of(band_of(0, m))] = part
+                elif m == q and q > 2:
+                    psend[q - 1] = packed(part)
                 else:
                     gsend[q, m] = part
         if q_list == (3, 4):
@@ -408,8 +457,7 @@
     make_and_send((2,), 0, 2)
     make_right(3)
     make_right(4)
-    make_and_send((3, 4), 2, 4)
-    make_and_send((3, 4), 4, 5)
+    make_and_send((3, 4), 2, 5)
     make_and_send((2,), 2, 5)
     make_and_send((1,), 2, 5)
     make_and_send((0,), 2, 5)
@@ -417,13 +465,18 @@
     for q_list, m_from, m_to in (
         ((1,), 0, 2),
         ((3, 4), 0, 2),
-        ((1,), 2, 4),
+        ((1,), 2, 3),
+        ((1,), 3, 4),
         ((1,), 4, 5),
         ((2,), 0, 2),
-        ((3, 4), 2, 4),
-        ((2,), 2, 4),
+        ((3, 4), 2, 3),
+        ((2,), 2, 3),
+        ((2,), 3, 4),
         ((2,), 4, 5),
-        ((3, 4), 4, 5),
+        ((4,), 3, 4),
+        ((3,), 4, 5),
+        ((3,), 3, 4),
+        ((4,), 4, 5),
     ):
         for q in q_list:
 
@@ -431,7 +484,11 @@
             def _():
                 set_arrival(q, m_from, m_to).wait_recv()
                 for m in range(m_from, m_to):
-                    out[:, lanes_of(band_of(q, m))] += grecv[q, m]
+                    o = lanes_of(band_of(q, m))
+                    if q > 2 and m == OPPOSITE[q]:
+                        out[:, o] += unpacked(precv[q - 1])
+                    else:
+                        out[:, o] += grecv[q, m]
 
     for q in range(1, NEAR):
 
@@ -469,13 +526,16 @@
                 pltpu.VMEM((2, NEAR * LANES, BLOCKS * FINE), BF16),
                 pltpu.VMEM((NEAR, NEAR, LANES, LANES), F32),
                 pltpu.VMEM((NEAR, NEAR, LANES, LANES), F32),
+                pltpu.VMEM((NEAR - 1, FINE + 8, LANES), F32),
+                pltpu.VMEM((NEAR - 1, FINE + 8, LANES), F32),
                 dma((2,)),
                 dma,
                 dma((3,)),
                 dma((NEAR - 1,)),
                 dma((NEAR - 1, 2)),
                 dma((NEAR - 1,)),
-                dma((NEAR - 1, 3)),
+                dma((NEAR - 1,)),
+                dma((NEAR - 1, 4)),
             ],
             compiler_params=pltpu.CompilerParams(
                 collective_id=0, has_side_effects=True, vmem_limit_bytes=40 << 20

time: 19.7 us -> 19.5 us (0.990)
  the two profiles are of different devices: /device:TPU:24 before, /device:TPU:25 now
where the time goes in v6:
time: 19.5 us; the launch traced here: 19.4 us
  Pallas kernels  18.5 us (95%)
  local copies, waits for them, and re-layouts  0.9 us (5%)
    pallas_call x1, Pallas kernels, body(): pl.pallas_call(lambda *refs: kernel(rows, cols, *refs), out_shape=jax.Sha...  18.5 us
    unnamed x1, local copies, waits for them, and re-layouts  0.9 us

profile of v6, /device:TPU:25, one launch (start us, length us, event | category | flops | bytes accessed | tf_op | source)
XLA Modules:
  0.0 19.4 jit_solution(11884343081461833136)
XLA Ops:
  0.0 18.5 %shard_map.55 = f32[128,1664]{1,0:T(8,128)S(1)} custom-call(f32[20,8,4096]{2,1,0:T(8,128)} %bitcast.3, s32[8,20]{1,0:T(8,128)} %refs_1_.1, s32[8,5]{1,0:T(8,128)} %refs_2_.1, f32[8,4096]{1,0:T(8,128)} %refs_3_.1, s32[1024]{0:T(1024)} %refs_4_.1), custom_call_target="tpu_custom_call" | custom-call | tf_op jit(solution)/shard_map/pallas_call | solution.py:507
  18.5 0.9 %copy.7 = f32[2,64,1664]{2,1,0:T(8,128)} copy(f32[2,64,1664]{2,1,0:T(8,128)S(1)} %bitcast.2) | data formatting | bytes 1703936

commit v7 on v6

--- a/solution.py
+++ b/solution.py
@@ -315,7 +315,7 @@
     def piece_copy(q, m, group):
         to = OPPOSITE[q]
         recv_sem = grecv_sem.at[to - 1, max(m - 1, 0)]
-        if m == q and q > 2:
+        if m == q and q > 1:
             return pltpu.make_async_remote_copy(
                 src_ref=psend.at[q - 1],
                 dst_ref=precv.at[to - 1],
@@ -335,7 +335,7 @@
         )
 
     def set_arrival(q, m_from, m_to):
-        alone = m_from == OPPOSITE[q] and q > 2
+        alone = m_from == OPPOSITE[q] and q > 1
         return pltpu.make_async_remote_copy(
             src_ref=psend.at[q - 1] if alone else gsend.at[q, m_from:m_to],
             dst_ref=precv.at[q - 1] if alone else grecv.at[q, m_from:m_to],
@@ -355,14 +355,14 @@
             device_id_type=MESH,
         ).wait_send()
         pltpu.make_async_remote_copy(
-            src_ref=gsend.at[q, 0:4] if q > 2 else gsend.at[q],
-            dst_ref=grecv.at[q, 0:4] if q > 2 else grecv.at[q],
+            src_ref=gsend.at[q, 0:4] if q > 1 else gsend.at[q],
+            dst_ref=grecv.at[q, 0:4] if q > 1 else grecv.at[q],
             send_sem=gsend_sem.at[q - 1],
             recv_sem=grecv_sem.at[q - 1, 0],
             device_id=places[q],
             device_id_type=MESH,
         ).wait_send()
-        if q > 2:
+        if q > 1:
             piece_copy(q, q, None).wait_send()
 
     def start_pieces(q, m_from, m_to, group):
@@ -378,7 +378,7 @@
                 part = g[at * LANES : (at + 1) * LANES, (m - m_from) * LANES : (m - m_from + 1) * LANES]
                 if q == 0:
                     out[:, lanes_of(band_of(0, m))] = part
-                elif m == q and q > 2:
+                elif m == q and q > 1:
                     psend[q - 1] = packed(part)
                 else:
                     gsend[q, m] = part
@@ -485,7 +485,7 @@
                 set_arrival(q, m_from, m_to).wait_recv()
                 for m in range(m_from, m_to):
                     o = lanes_of(band_of(q, m))
-                    if q > 2 and m == OPPOSITE[q]:
+                    if q > 1 and m == OPPOSITE[q]:
                         out[:, o] += unpacked(precv[q - 1])
                     else:
                         out[:, o] += grecv[q, m]

time: 19.5 us -> 19.2 us (0.985)
  Pallas kernels: 18.5 us -> 18.2 us
    pallas_call x1, Pallas kernels: 18.5 us -> 18.2 us  [body(): pl.pallas_call(lambda *refs: kernel(rows, cols, *refs), out_shape=jax.Sha...]
where the time goes in v7:
time: 19.2 us; the launch traced here: 19.1 us
  Pallas kernels  18.2 us (95%)
  local copies, waits for them, and re-layouts  0.9 us (5%)
    pallas_call x1, Pallas kernels, body(): pl.pallas_call(lambda *refs: kernel(rows, cols, *refs), out_shape=jax.Sha...  18.2 us
    unnamed x1, local copies, waits for them, and re-layouts  0.9 us

profile of v7, /device:TPU:25, one launch (start us, length us, event | category | flops | bytes accessed | tf_op | source)
XLA Modules:
  0.0 19.1 jit_solution(18251291722397537797)
XLA Ops:
  0.0 18.2 %shard_map.55 = f32[128,1664]{1,0:T(8,128)S(1)} custom-call(f32[20,8,4096]{2,1,0:T(8,128)} %bitcast.3, s32[8,20]{1,0:T(8,128)} %refs_1_.1, s32[8,5]{1,0:T(8,128)} %refs_2_.1, f32[8,4096]{1,0:T(8,128)} %refs_3_.1, s32[1024]{0:T(1024)} %refs_4_.1), custom_call_target="tpu_custom_call" | custom-call | tf_op jit(solution)/shard_map/pallas_call | solution.py:507
  18.2 0.9 %copy.7 = f32[2,64,1664]{2,1,0:T(8,128)} copy(f32[2,64,1664]{2,1,0:T(8,128)S(1)} %bitcast.2) | data formatting | bytes 1703936

commit v8 on v7

--- a/solution.py
+++ b/solution.py
@@ -171,22 +171,25 @@
             tpack[0, group, pair, pl.ds(0, CHUNKS, 2), :] = jnp.where(low_half, a, pltpu.roll(b, FINE, 1))
             tpack[0, group, pair, pl.ds(1, CHUNKS, 2), :] = jnp.where(low_half, pltpu.roll(a, FINE, 1), b)
 
+    def tile_sem(q, group):
+        return 2 * (q - 2) + group if q > 2 else q - 1
+
     def tile_copy(q, group):
         return pltpu.make_async_remote_copy(
             src_ref=tpack.at[0, group],
             dst_ref=tpack.at[OPPOSITE[q], group],
             send_sem=tsend.at[q - 1],
-            recv_sem=trecv.at[OPPOSITE[q] - 1, group],
+            recv_sem=trecv.at[tile_sem(OPPOSITE[q], group)],
             device_id=places[q],
             device_id_type=MESH,
         )
 
     def arrival(q, group):
         return pltpu.make_async_remote_copy(
-            src_ref=tpack.at[0, group],
-            dst_ref=tpack.at[q, group],
+            src_ref=tpack.at[0, group] if q > 2 else tpack.at[0],
+            dst_ref=tpack.at[q, group] if q > 2 else tpack.at[q],
             send_sem=tsend.at[q - 1],
-            recv_sem=trecv.at[q - 1, group],
+            recv_sem=trecv.at[tile_sem(q, group)],
             device_id=places[q],
             device_id_type=MESH,
         )
@@ -312,9 +315,12 @@
             [jnp.concatenate([a, b], axis=1), jnp.concatenate([b_t, c], axis=1)], axis=0
         )
 
+    def set_sem(q, m):
+        return 0 if q == 1 else 1 + 4 * (q - 2) + max(m - 1, 0)
+
     def piece_copy(q, m, group):
         to = OPPOSITE[q]
-        recv_sem = grecv_sem.at[to - 1, max(m - 1, 0)]
+        recv_sem = grecv_sem.at[set_sem(to, m)]
         if m == q and q > 1:
             return pltpu.make_async_remote_copy(
                 src_ref=psend.at[q - 1],
@@ -340,7 +346,7 @@
             src_ref=psend.at[q - 1] if alone else gsend.at[q, m_from:m_to],
             dst_ref=precv.at[q - 1] if alone else grecv.at[q, m_from:m_to],
             send_sem=gsend_sem.at[q - 1],
-            recv_sem=grecv_sem.at[q - 1, max(m_from - 1, 0)],
+            recv_sem=grecv_sem.at[set_sem(q, m_from)],
             device_id=places[q],
             device_id_type=MESH,
         )
@@ -350,7 +356,7 @@
             src_ref=tpack.at[0],
             dst_ref=tpack.at[OPPOSITE[q]],
             send_sem=tsend.at[q - 1],
-            recv_sem=trecv.at[q - 1, 0],
+            recv_sem=trecv.at[tile_sem(q, 0)],
             device_id=places[q],
             device_id_type=MESH,
         ).wait_send()
@@ -358,7 +364,7 @@
             src_ref=gsend.at[q, 0:4] if q > 1 else gsend.at[q],
             dst_ref=grecv.at[q, 0:4] if q > 1 else grecv.at[q],
             send_sem=gsend_sem.at[q - 1],
-            recv_sem=grecv_sem.at[q - 1, 0],
+            recv_sem=grecv_sem.at[set_sem(q, 0)],
             device_id=places[q],
             device_id_type=MESH,
         ).wait_send()
@@ -441,10 +447,8 @@
     lax.fori_loop(0, BLOCKS, spread_near, 0)
     smooth(0)
     wait_tiles(1, 0)
-    wait_tiles(1, 1)
     smooth(1)
-    make_and_send((1,), 0, 2)
-    make_and_send((0,), 0, 2)
+    make_and_send((0, 1), 0, 2)
     for group in range(2):
         wait_tiles(3, group)
         wait_tiles(4, group)
@@ -452,23 +456,18 @@
         smooth_half(4, group)
         make_and_send_halves(group, 0, 2)
     wait_tiles(2, 0)
-    wait_tiles(2, 1)
     smooth(2)
     make_and_send((2,), 0, 2)
     make_right(3)
     make_right(4)
     make_and_send((3, 4), 2, 5)
     make_and_send((2,), 2, 5)
-    make_and_send((1,), 2, 5)
-    make_and_send((0,), 2, 5)
+    make_and_send((0, 1), 2, 5)
 
     for q_list, m_from, m_to in (
-        ((1,), 0, 2),
         ((3, 4), 0, 2),
-        ((1,), 2, 3),
-        ((1,), 3, 4),
-        ((1,), 4, 5),
         ((2,), 0, 2),
+        ((1,), 0, 5),
         ((3, 4), 2, 3),
         ((2,), 2, 3),
         ((2,), 3, 4),
@@ -532,10 +531,10 @@
                 dma,
                 dma((3,)),
                 dma((NEAR - 1,)),
-                dma((NEAR - 1, 2)),
+                dma((6,)),
                 dma((NEAR - 1,)),
                 dma((NEAR - 1,)),
-                dma((NEAR - 1, 4)),
+                dma((13,)),
             ],
             compiler_params=pltpu.CompilerParams(
                 collective_id=0, has_side_effects=True, vmem_limit_bytes=40 << 20

time: 19.2 us -> 19.2 us (level)
  no operation moved by 1% of the time
where the time goes in v8:
time: 19.2 us; the launch traced here: 19 us
  Pallas kernels  18.1 us (94%)
  local copies, waits for them, and re-layouts  0.9 us (5%)
    pallas_call x1, Pallas kernels, body(): pl.pallas_call(lambda *refs: kernel(rows, cols, *refs), out_shape=jax.Sha...  18.1 us
    unnamed x1, local copies, waits for them, and re-layouts  0.9 us

profile of v8, /device:TPU:25, one launch (start us, length us, event | category | flops | bytes accessed | tf_op | source)
XLA Modules:
  0.0 19.0 jit_solution(9040891484536658290)
XLA Ops:
  0.0 18.1 %shard_map.55 = f32[128,1664]{1,0:T(8,128)S(1)} custom-call(f32[20,8,4096]{2,1,0:T(8,128)} %bitcast.3, s32[8,20]{1,0:T(8,128)} %refs_1_.1, s32[8,5]{1,0:T(8,128)} %refs_2_.1, f32[8,4096]{1,0:T(8,128)} %refs_3_.1, s32[1024]{0:T(1024)} %refs_4_.1), custom_call_target="tpu_custom_call" | custom-call | tf_op jit(solution)/shard_map/pallas_call | solution.py:506
  18.1 0.9 %copy.7 = f32[2,64,1664]{2,1,0:T(8,128)} copy(f32[2,64,1664]{2,1,0:T(8,128)S(1)} %bitcast.2) | data formatting | bytes 1703936

commit v9 on v8

--- a/solution.py
+++ b/solution.py
@@ -460,15 +460,15 @@
     make_and_send((2,), 0, 2)
     make_right(3)
     make_right(4)
-    make_and_send((3, 4), 2, 5)
+    make_and_send((3, 4), 3, 5)
     make_and_send((2,), 2, 5)
+    make_and_send((3, 4), 2, 3)
     make_and_send((0, 1), 2, 5)
 
     for q_list, m_from, m_to in (
         ((3, 4), 0, 2),
         ((2,), 0, 2),
         ((1,), 0, 5),
-        ((3, 4), 2, 3),
         ((2,), 2, 3),
         ((2,), 3, 4),
         ((2,), 4, 5),
@@ -476,6 +476,7 @@
         ((3,), 4, 5),
         ((3,), 3, 4),
         ((4,), 4, 5),
+        ((3, 4), 2, 3),
     ):
         for q in q_list:
 

time: 19.2 us -> 19.2 us (level)
  no operation moved by 1% of the time
where the time goes in v9:
time: 19.2 us; the launch traced here: 19.1 us
  Pallas kernels  18.2 us (95%)
  local copies, waits for them, and re-layouts  0.9 us (5%)
    pallas_call x1, Pallas kernels, body(): pl.pallas_call(lambda *refs: kernel(rows, cols, *refs), out_shape=jax.Sha...  18.2 us
    unnamed x1, local copies, waits for them, and re-layouts  0.9 us

profile of v9, /device:TPU:25, one launch (start us, length us, event | category | flops | bytes accessed | tf_op | source)
XLA Modules:
  0.0 19.1 jit_solution(3732091882409981301)
XLA Ops:
  0.0 18.2 %shard_map.55 = f32[128,1664]{1,0:T(8,128)S(1)} custom-call(f32[20,8,4096]{2,1,0:T(8,128)} %bitcast.3, s32[8,20]{1,0:T(8,128)} %refs_1_.1, s32[8,5]{1,0:T(8,128)} %refs_2_.1, f32[8,4096]{1,0:T(8,128)} %refs_3_.1, s32[1024]{0:T(1024)} %refs_4_.1), custom_call_target="tpu_custom_call" | custom-call | tf_op jit(solution)/shard_map/pallas_call | solution.py:507
  18.2 0.9 %copy.7 = f32[2,64,1664]{2,1,0:T(8,128)} copy(f32[2,64,1664]{2,1,0:T(8,128)S(1)} %bitcast.2) | data formatting | bytes 1703936
